TPU v7x, 32 devices: a whole 2x2x4 slice. The times are simulated.
32 devices in a mesh: dp: 16 (over z, x, core), head: 2 (over y).
Axes of the slice: x: 2, y: 2, z: 4, core: 2. Of those that a mesh axis runs over, the one named last changes fastest.
Arguments:
- block_in: bfloat16 [16, 1024, 768], P('dp', 'head'), may hold values from -8 to 8
- text: bfloat16 [16, 256, 1024], P('dp'), may hold values from -6 to 6
- timesteps: int32 [16], P('dp'), may hold values from 0 to 999
- frame_mask: int32 [16, 1024], P('dp'), may hold values from 0 to 1, as said below
- text_mask: int32 [16, 256], P('dp'), may hold values from 0 to 1, as said below
- cotangent: bfloat16 [16, 1024, 768], P('dp', 'head'), may hold values from -6 to 6
- w_ada: float32 [768, 4608], P(('dp', 'head')), may hold values from -0.625 to 0.625
- w_qkv: float32 [768, 2304], P(('dp', 'head')), may hold values from -0.21875 to 0.21875
- w_out: float32 [768, 768], P(('dp', 'head')), may hold values from -3.5 to 3.5
- w_cq: float32 [768, 768], P(('dp', 'head')), may hold values from -0.21875 to 0.21875
- w_cout: float32 [768, 768], P(('dp', 'head')), may hold values from -1.75 to 1.75
- w_ckv: float32 [1024, 2, 768], P('dp', None, 'head'), may hold values from -0.1875 to 0.1875
- w_fc1: float32 [768, 3072], P('dp', 'head'), may hold values from -0.21875 to 0.21875
- w_fc2: float32 [3072, 768], P('head', 'dp'), may hold values from -0.109375 to 0.109375
- row_state: float32 [8704], replicated, may hold values from 2.2439396e-08 to 5.983839e-07, as said below
- col_state: float32 [14592], replicated, may hold values from 2.2439396e-08 to 5.983839e-07, as said below
Outputs:
- block_out: bfloat16 [16, 1024, 768], P('dp', 'head')
- input_grad: bfloat16 [16, 1024, 768], P('dp', 'head')
- grad_norm: float32 [], replicated
- row_new: float32 [8704], replicated
- col_new: float32 [14592], replicated
- grad_ada: float32 [768, 4608], P(('dp', 'head'))
- grad_qkv: float32 [768, 2304], P(('dp', 'head'))
- grad_out: float32 [768, 768], P(('dp', 'head'))
- grad_cq: float32 [768, 768], P(('dp', 'head'))
- grad_cout: float32 [768, 768], P(('dp', 'head'))
- grad_ckv: float32 [1024, 2, 768], P('dp', None, 'head')
- grad_fc1: float32 [768, 3072], P('dp', 'head')
- grad_fc2: float32 [3072, 768], P('head', 'dp')
- new_ada: float32 [768, 4608], P(('dp', 'head'))
- new_qkv: float32 [768, 2304], P(('dp', 'head'))
- new_out: float32 [768, 768], P(('dp', 'head'))
- new_cq: float32 [768, 768], P(('dp', 'head'))
- new_cout: float32 [768, 768], P(('dp', 'head'))
- new_ckv: float32 [1024, 2, 768], P('dp', None, 'head')
- new_fc1: float32 [768, 3072], P('dp', 'head')
- new_fc2: float32 [3072, 768], P('head', 'dp')
Inputs may be any that keep to these rules, and one draw needn't show every extreme that they name: `frame_mask`: each clip's frame mask is 1 on a prefix of 256 to 1024 frames and 0 after it; in each aligned block of 4 clips, one clip has all 1024 frames. `text_mask`: each clip's text mask is 1 on a prefix of 77 to 256 tokens and 0 after it; some clip has 77 tokens and some has 256. `row_state`: Positive. `col_state`: Positive.
All inputs are finite; a program needn't handle non-finite values.
Results may differ from a plain program's by a relative error of at most 0.023.
The roundings to bfloat16 on the way count: a program that leaves them out, or rounds other values in their place, can miss the bound.
Values may be sent and summed in bfloat16 or wider, within the bound.
No kernel may reach another device: no remote copies, remote signals or barrier semaphores. Data moves between devices by JAX's collectives and lax.ppermute only.
A program may use at most 192 MiB of HBM per device.

v0:
```python
import functools

import jax
import jax.numpy as jnp
from jax import lax
from jax.experimental import pallas as pl
from jax.experimental.pallas import tpu as pltpu
from jax.sharding import PartitionSpec as P

D = 768
FF = 3072
DT = 1024
HD = 64
HALF = FF // 2

PRECISE = lax.Precision.HIGHEST
FLOAT = jnp.float32
BFLOAT = jnp.bfloat16
EPS_NORM = 1e-06
EPS_FACTOR = 1e-30
CLIP_NORM = 1.0
CLIP_UPDATE = 0.25
DECAY_RATE = 0.5
RELATIVE_RATE = 4.0
SCALE_FLOOR = 0.001
SCORE_SCALE = 0.125
MASKED_SCORE = -1e30
DP = ("far", "near", "core")
ALL = DP + ("head",)
HEAD = ("head",)
PAIR = 2 * HD
PAIRS = D // PAIR


def embed_part(steps, first, count):
    halfway = D // 2
    place = first + jnp.arange(count)
    freqs = jnp.exp(-jnp.log(10000.0) * (place % halfway).astype(FLOAT) / halfway)
    angles = steps.astype(FLOAT)[:, None] * freqs
    waves = jnp.where(place < halfway, jnp.cos(angles), jnp.sin(angles))
    return jax.nn.silu(waves).astype(BFLOAT)


def core_link():
    return (DP, 1)


def row_link():
    return (HEAD, 1)


def far_links():
    masks, mask = [], 2
    while mask < lax.axis_size(DP):
        masks.append(mask)
        mask = mask * 2
    return [(DP, mask) for mask in masks]


def dp_bits():
    return lax.axis_size(DP).bit_length() - 1


def bit_of(link):
    return (lax.axis_index(link[0]) // link[1]) % 2


def cross(values, link):
    pairs = [(place, place ^ link[1]) for place in range(lax.axis_size(link[0]))]
    return lax.ppermute(values, link[0], pairs)


def dim_of(link, head):
    if link[0] == HEAD:
        return {"first": 0, "last": dp_bits(), "columns": dp_bits() + 1}[head]
    return (1 if head == "first" else 0) + dp_bits() - link[1].bit_length()


def leading(head):
    return dp_bits() + (0 if head == "columns" else 1)


def grow(block, link, head):
    other = cross(block, link)
    upper = bit_of(link) == 1
    low = jnp.where(upper, other, block)
    high = jnp.where(upper, block, other)
    return jnp.concatenate([low, high], axis=dim_of(link, head))


def shrink(block, link, head, kind=BFLOAT):
    dim, bit = dim_of(link, head), bit_of(link)
    half = block.shape[dim] // 2
    kept = lax.dynamic_slice_in_dim(block, bit * half, half, axis=dim)
    sent = lax.dynamic_slice_in_dim(block, (1 - bit) * half, half, axis=dim)
    return (kept.astype(FLOAT) + cross(sent.astype(BFLOAT), link).astype(FLOAT)).astype(kind)


class Chain:
    def __init__(self, state, steps):
        self.state, self.steps = state, list(steps)

    def advance(self, count=1):
        for _ in range(min(count, len(self.steps))):
            self.state = self.steps.pop(0)(self.state)
        return self

    def finish(self):
        return self.advance(len(self.steps)).state


def tie(chains, *values):
    states, values = lax.optimization_barrier(([chain.state for chain in chains], values))
    for chain, state in zip(chains, states):
        chain.state = state
    return values


def gather_chain(block, head, links):
    return Chain(block, [lambda state, link=link: grow(state, link, head) for link in links])


def with_bits(shard, head):
    return shard.reshape((1,) * leading(head) + shard.shape)


def scatter_chain(matrix, head, row_early):
    bits = leading(head)
    rows, columns = matrix.shape[-2:]
    split = dp_bits() if head == "first" else bits
    block = matrix.reshape((2,) * bits + (rows // 2**split, columns))
    far = far_links()
    plane = [far[0], row_link()] if row_early else [row_link(), far[0]]
    order = [core_link()] + plane + far[1:]
    kinds = [BFLOAT] * (len(order) - 1) + [FLOAT]
    steps = [
        lambda state, link=link, kind=kind: shrink(state, link, head, kind)
        for link, kind in zip(order, kinds)
    ]
    return Chain(block, steps + [lambda state: state.reshape(state.shape[bits:])])


def sum_all(values):
    for link in [core_link()] + far_links() + [row_link()]:
        values = values + cross(values, link)
    return values


def on_own_chip():
    return bit_of(core_link()) == bit_of(row_link())


def swap_only(values):
    pairs = []
    for place in range(lax.axis_size(DP)):
        for head in range(2):
            if place & 1 != head:
                pairs.append((place * 2 + head, ((place & ~1) | head) * 2 + (place & 1)))
    return lax.ppermute(values, ALL, pairs)


def swap_place(values):
    return jnp.where(on_own_chip(), values, swap_only(values))


def from_clip_core(values):
    pairs = []
    for place in range(0, lax.axis_size(DP), 2):
        for head in range(2):
            pairs.append(((place + head) * 2 + head, (place + 1 - head) * 2 + head))
    return jnp.where(on_own_chip(), values, lax.ppermute(values, ALL, pairs))


def nt(left, right):
    return lax.dot_general(left, right, (((1,), (1,)), ((), ())), preferred_element_type=FLOAT)


def nn(left, right):
    return lax.dot_general(left, right, (((1,), (0,)), ((), ())), preferred_element_type=FLOAT)


def lanes_of(length):
    return lax.broadcasted_iota(jnp.int32, (length, PAIR), 1)


def with_spare(pair, head, spare):
    lane = lanes_of(pair.shape[0])
    rest = jnp.where(lane == HD * (1 - head), spare, jnp.zeros_like(pair))
    return jnp.where(lane // HD == head, pair, rest)


def attend_kernel(blocks, *refs):
    query_ref, out_ref, log_ref = refs[0], refs[1 + 3 * blocks], refs[2 + 3 * blocks]
    ins = refs[1 : 1 + 3 * blocks]
    one = jnp.ones((1, 1), BFLOAT)
    for place in range(log_ref.shape[0]):
        columns = pl.ds(place * PAIR, PAIR)
        queries = query_ref[:, columns] * jnp.asarray(SCORE_SCALE, BFLOAT)
        values_t = [ref[:, columns].T for ref in ins[1::3]]
        results, logs = [], []
        for head in range(2):
            query = with_spare(queries, head, one)
            scores = [
                nt(with_spare(key_ref[:, columns], head, bias_ref[...]), query)
                for key_ref, bias_ref in zip(ins[0::3], ins[2::3])
            ]
            peak = functools.reduce(
                jnp.maximum, [jnp.max(score, axis=0, keepdims=True) for score in scores]
            )
            total = None
            for score, value_t in zip(scores, values_t):
                probs = jnp.exp(score - peak).astype(BFLOAT)
                row = lax.broadcasted_iota(jnp.int32, value_t.shape, 0)
                term = nn(jnp.where(row // HD == head, value_t, one), probs)
                total = term if total is None else total + term
            weight = total[HD * (1 - head) : HD * (1 - head) + 1, :]
            results.append(total[HD * head : HD * (head + 1), :] / weight)
            logs.append(peak + jnp.log(weight))
        out_ref[:, columns] = jnp.concatenate(results, axis=0).T.astype(BFLOAT)
        log_ref[place] = jnp.concatenate(logs, axis=0)


def back_kernel(blocks, places, *refs):
    query_ref, out_ref, grad_ref, log_ref = refs[:4]
    ins = refs[4 : 4 + 3 * blocks]
    query_grad_ref, pair_grad_refs = refs[4 + 3 * blocks], refs[5 + 3 * blocks :]
    zero = jnp.zeros((1, 1), BFLOAT)
    one = jnp.ones((1, 1), BFLOAT)
    chooser = (
        lax.broadcasted_iota(jnp.int32, (8, PAIR), 1) // HD
        == lax.broadcasted_iota(jnp.int32, (8, PAIR), 0)
    ).astype(FLOAT)
    count = log_ref.shape[0]
    for place in range(count):
        columns = pl.ds(place * PAIR, PAIR)
        queries = query_ref[:, columns] * jnp.asarray(SCORE_SCALE, BFLOAT)
        out_grad = grad_ref[:, columns]
        product = out_ref[:, columns].astype(FLOAT) * out_grad.astype(FLOAT)
        inner = lax.dot_general(
            chooser,
            product,
            (((1,), (1,)), ((), ())),
            precision=PRECISE,
            preferred_element_type=FLOAT,
        )
        query_parts = [None, None]
        for block in range(blocks):
            keys, values = ins[3 * block][:, columns], ins[3 * block + 1][:, columns]
            bias, keys_t = ins[3 * block + 2][...], keys.T
            key_grad, value_grad = None, None
            for head in range(2):
                grad_here = with_spare(out_grad, head, zero)
                score = nt(with_spare(keys, head, bias), with_spare(queries, head, one))
                probs = jnp.exp(score - log_ref[place, head : head + 1, :])
                prob_grad = nt(values, grad_here)
                score_grad = (probs * (prob_grad - inner[head : head + 1, :])).astype(BFLOAT)
                value_term = nn(probs.astype(BFLOAT), grad_here)
                key_term = nn(score_grad, with_spare(queries, head, zero))
                query_term = nn(keys_t[HD * head : HD * (head + 1), :], score_grad)
                value_grad = value_term if value_grad is None else value_grad + value_term
                key_grad = key_term if key_grad is None else key_grad + key_term
                query_parts[head] = (
                    query_term if query_parts[head] is None else query_parts[head] + query_term
                )
            key_at, value_at = places(pl.program_id(0) * count + place)
            key_at = pl.multiple_of(key_at * PAIR, PAIR)
            value_at = pl.multiple_of(value_at * PAIR, PAIR)
            pair_grad_refs[block][:, pl.ds(key_at, PAIR)] = key_grad.astype(BFLOAT)
            pair_grad_refs[block][:, pl.ds(value_at, PAIR)] = value_grad.astype(BFLOAT)
        joined = jnp.concatenate(query_parts, axis=0) * SCORE_SCALE
        query_grad_ref[:, columns] = joined.T.astype(BFLOAT)


def column_block(length, count):
    return pl.BlockSpec((length, PAIR * count), lambda step: (0, step))


def plain_places(pair):
    return pair, pair + PAIRS


def half_places(pair):
    half, part = pair // (PAIRS // 2), pair % (PAIRS // 2)
    return half * PAIRS + part, half * PAIRS + PAIRS // 2 + part


def whole_block(shape):
    return pl.BlockSpec(shape, lambda pair: (0,) * len(shape))


def log_block(frames, count):
    return pl.BlockSpec((count, 2, frames), lambda step: (step, 0, 0))


def key_specs(key_values, places, count):
    specs, operands = [], []
    for joint, bias in key_values:
        length = joint.shape[0]
        specs += [
            pl.BlockSpec(
                (length, PAIR * count), lambda step: (0, places(step * count)[0] // count)
            ),
            pl.BlockSpec(
                (length, PAIR * count), lambda step: (0, places(step * count)[1] // count)
            ),
            whole_block((length, PAIR)),
        ]
        operands += [joint, joint, bias]
    return specs, operands


def room(mebibytes):
    return pltpu.CompilerParams(vmem_limit_bytes=mebibytes * 1024 * 1024)


LIGHT = pl.CostEstimate(flops=1000, bytes_accessed=1000, transcendentals=0)


def attend(queries, key_values, places, count=1):
    frames, blocks = queries.shape[0], len(key_values)
    specs, operands = key_specs(key_values, places, count)
    return pl.pallas_call(
        functools.partial(attend_kernel, blocks),
        grid=(PAIRS // count,),
        in_specs=[column_block(frames, count)] + specs,
        out_specs=[column_block(frames, count), log_block(frames, count)],
        out_shape=[
            jax.ShapeDtypeStruct((frames, D), BFLOAT),
            jax.ShapeDtypeStruct((PAIRS, 2, frames), FLOAT),
        ],
        compiler_params=room(48),
        cost_estimate=LIGHT,
    )(queries, *operands)


def attend_back(queries, out, out_grad, logs, key_values, places, count=1):
    frames, blocks = queries.shape[0], len(key_values)
    specs, operands = key_specs(key_values, places, count)
    return pl.pallas_call(
        functools.partial(back_kernel, blocks, places),
        grid=(PAIRS // count,),
        in_specs=[column_block(frames, count)] * 3 + [log_block(frames, count)] + specs,
        out_specs=[column_block(frames, count)] + [whole_block(joint.shape) for joint, _ in key_values],
        out_shape=[jax.ShapeDtypeStruct((frames, D), BFLOAT)]
        + [jax.ShapeDtypeStruct(joint.shape, BFLOAT) for joint, _ in key_values],
        compiler_params=room(48),
        cost_estimate=LIGHT,
    )(queries, out, out_grad, logs, *operands)


def outer_kernel(*refs):
    out_ref, count = refs[-1], len(refs) // 2
    at = 0
    for place in range(count):
        left, right = refs[2 * place], refs[2 * place + 1]
        width = right.shape[1]
        product = lax.dot_general(
            left[...], right[...], (((0,), (0,)), ((), ())), preferred_element_type=FLOAT
        )
        out_ref[:, at : at + width] = product.astype(BFLOAT)
        at += width


def outer(*pairs):
    operands = [matrix for pair in pairs for matrix in pair]
    shape = (pairs[0][0].shape[1], sum(right.shape[1] for _, right in pairs))
    return pl.pallas_call(
        outer_kernel,
        out_shape=jax.ShapeDtypeStruct(shape, BFLOAT),
        compiler_params=room(48),
        cost_estimate=LIGHT,
    )(*operands)


def bias_of(allowed):
    column = jnp.where(allowed > 0, 0.0, MASKED_SCORE).astype(BFLOAT)
    return jnp.broadcast_to(column[:, None], (allowed.shape[0], PAIR))


LINE = 128
ROW_SIZES = [D, D, D, D, D, DT, D, FF]
COL_SIZES = [6 * D, 3 * D, D, D, D, 2 * D, FF, D]
ROW_LINES = sum(ROW_SIZES) // LINE
COL_LINES = sum(COL_SIZES) // LINE
STAT_LINES = ROW_LINES + COL_LINES + 2


def starts_of(sizes, first):
    starts = []
    for size in sizes:
        starts.append(first)
        first += size // LINE
    return starts


ROW_STARTS = starts_of(ROW_SIZES, 0)
COL_STARTS = starts_of(COL_SIZES, ROW_LINES)


def lines_at(line, shape):
    return lax.broadcasted_iota(jnp.int32, shape, 1) + line * LINE


def down_lines(column, offset, lines):
    shape = (column.shape[0], LINE)
    wanted = lax.broadcasted_iota(jnp.int32, shape, 0) + offset
    return [
        jnp.sum(jnp.where(lines_at(line, shape) == wanted, column, 0.0), axis=0, keepdims=True)
        for line in range(lines)
    ]


def from_lines(lines, offset, count):
    shape = (count, LINE)
    wanted = lax.broadcasted_iota(jnp.int32, shape, 0) + offset
    total = jnp.zeros(shape, FLOAT)
    for line in range(lines.shape[0]):
        here = jnp.where(lines_at(line, shape) == wanted, lines[line : line + 1, :], 0.0)
        total = total + here
    return jnp.sum(total, axis=1, keepdims=True)


def pieces_of(grad_refs):
    ada, query_out, key_value, cross_pair, text_pair, mlp = grad_refs
    return [
        [(ada, 0, 6 * D)],
        [(query_out, 0, D), (key_value, 0, 2 * D)],
        [(query_out, D, D)],
        [(cross_pair, 0, D)],
        [(cross_pair, D, D)],
        [(text_pair, 0, D)],
        [(mlp.at[0], 0, HALF)],
        [(mlp.at[1], 0, HALF)],
    ]


def joined_pieces(refs):
    square, text_pair, mlp = refs
    parts, at = [], 0
    for place in range(5):
        parts.append((square, at, COL_SIZES[place]))
        at += COL_SIZES[place]
    return parts + [(text_pair, 0, D), (mlp, 0, HALF), (mlp, HALF, HALF)]


def statistics_kernel(place_ref, weight_ref, *refs):
    grad_refs, out_ref = refs[:6], refs[6]
    data_at, head_at = place_ref[0], place_ref[1]
    flat_at = data_at * 2 + head_at
    out_ref[STAT_LINES - 2 : STAT_LINES - 1, :] = weight_ref[...]
    out_ref[STAT_LINES - 1 : STAT_LINES, :] = jnp.zeros((1, LINE), FLOAT)
    for place, parts in enumerate(pieces_of(grad_refs)):
        across, down = 0.0, []
        for ref, first, columns in parts:
            rows = ref.shape[0]
            wide = jnp.zeros((rows, LINE), FLOAT)
            for line in range(columns // LINE):
                piece = ref[:, first + line * LINE : first + (line + 1) * LINE]
                square = piece * piece
                wide = wide + square
                down.append(jnp.sum(square, axis=0, keepdims=True))
            across = across + jnp.sum(wide, axis=1, keepdims=True)
        offset = (flat_at if place < 5 else data_at) * rows
        row_start, col_start = ROW_STARTS[place], COL_STARTS[place]
        if place == 7:
            row_start, col_start = col_start, row_start
        row_lines = (COL_SIZES if place == 7 else ROW_SIZES)[place] // LINE
        for line, entry in enumerate(down_lines(across, offset, row_lines)):
            out_ref[row_start + line : row_start + line + 1, :] = entry
        groups = {5: 2}.get(place, 1)
        size = len(down) // groups
        for line, entry in enumerate(down):
            if place < 5:
                out_ref[col_start + line : col_start + line + 1, :] = entry
            else:
                for half in range(2):
                    at = col_start + (line // size * 2 + half) * size + line % size
                    out_ref[at : at + 1, :] = jnp.where(head_at == half, entry, 0.0)


def lane_of(lines, lane):
    shape = (1, LINE)
    here = lax.broadcasted_iota(jnp.int32, shape, 1) == lane
    return jnp.sum(jnp.where(here, lines, 0.0), axis=1, keepdims=True)


def update_kernel(place_ref, sums_ref, row_ref, col_ref, *refs):
    grad_refs, outs = refs[:6], refs[6:]
    row_out, col_out, norm_out, total_out = outs[:4]
    clipped_refs, update_refs = outs[4:12], joined_pieces(outs[12:15])
    data_at, head_at = place_ref[0], place_ref[1]
    flat_at = data_at * 2 + head_at
    row_sums = sums_ref[0:ROW_LINES, :]
    square_total = jnp.sum(jnp.sum(row_sums, axis=0, keepdims=True), axis=1, keepdims=True)
    norm = jnp.sqrt(square_total)
    factor = 1.0 / jnp.maximum(1.0, norm / CLIP_NORM)
    norm_out[...] = jnp.broadcast_to(norm, (1, LINE))
    square_factor = factor * factor
    lane = lax.broadcasted_iota(jnp.int32, (1, LINE), 1)
    totals = jnp.zeros((1, LINE), FLOAT)
    for place, parts in enumerate(pieces_of(grad_refs)):
        rows_len, cols_len = ROW_SIZES[place], COL_SIZES[place]
        row_from, row_to = ROW_STARTS[place], ROW_STARTS[place] + rows_len // LINE
        col_from, col_to = COL_STARTS[place], COL_STARTS[place] + cols_len // LINE
        new_row = DECAY_RATE * row_ref[row_from:row_to, :] + (1.0 - DECAY_RATE) * (
            square_factor * sums_ref[row_from:row_to, :] / float(cols_len) + EPS_FACTOR
        )
        col_from, col_to = col_from - ROW_LINES, col_to - ROW_LINES
        new_col = DECAY_RATE * col_ref[col_from:col_to, :] + (1.0 - DECAY_RATE) * (
            square_factor
            * sums_ref[ROW_LINES + col_from : ROW_LINES + col_to, :]
            / float(rows_len)
            + EPS_FACTOR
        )
        row_out[row_from:row_to, :] = new_row
        col_out[col_from:col_to, :] = new_col
        row_mean = (
            jnp.sum(jnp.sum(new_row, axis=0, keepdims=True), axis=1, keepdims=True) / rows_len
        )
        rows = parts[0][0].shape[0]
        offset = (flat_at if place < 5 else data_at) * rows
        if place == 7:
            down = lax.rsqrt(from_lines(new_col, offset, rows))
            across = jnp.where(head_at == 0, new_row[:12], new_row[12:])
            across = lax.rsqrt(across / row_mean)
        else:
            down = lax.rsqrt(from_lines(new_row, offset, rows) / row_mean)
            if place == 5:
                keys = jnp.where(head_at == 0, new_col[0:3], new_col[3:6])
                values = jnp.where(head_at == 0, new_col[6:9], new_col[9:12])
                across = lax.rsqrt(jnp.concatenate([keys, values], axis=0))
            elif place == 6:
                across = lax.rsqrt(jnp.where(head_at == 0, new_col[:12], new_col[12:]))
            else:
                across = lax.rsqrt(new_col)
        square = jnp.zeros((rows, LINE), FLOAT)
        line_at = 0
        for ref, first, columns in parts:
            for line in range(columns // LINE):
                piece = ref[:, first + line * LINE : first + (line + 1) * LINE] * factor
                update = piece * (down * across[line_at : line_at + 1, :])
                clipped_refs[place][:, line_at * LINE : (line_at + 1) * LINE] = piece
                update_ref, update_at, _ = update_refs[place]
                update_at += line_at * LINE
                update_ref[:, update_at : update_at + LINE] = update
                square = square + update * update
                line_at += 1
        total = jnp.sum(jnp.sum(square, axis=0, keepdims=True), axis=1, keepdims=True)
        totals = jnp.where(lane == place, total, totals)
    total_out[...] = totals


def apply_kernel(total_ref, weight_ref, *refs):
    master_refs, update_refs = joined_pieces(refs[:3]), joined_pieces(refs[3:6])
    for place in range(8):
        entries = float(ROW_SIZES[place] * COL_SIZES[place])
        total = lane_of(total_ref[...], place)
        weight = lane_of(weight_ref[...], place)
        limit = jnp.maximum(1.0, jnp.sqrt(total / entries) / CLIP_UPDATE)
        rate = RELATIVE_RATE * jnp.maximum(SCALE_FLOOR, jnp.sqrt(weight / entries))
        scale = rate / limit
        ref, at, columns = master_refs[place]
        update = update_refs[place][0][:, at : at + columns]
        refs[6 + place][...] = ref[:, at : at + columns] - scale * update


def weight_kernel(*refs):
    lane = lax.broadcasted_iota(jnp.int32, (1, LINE), 1)
    totals = jnp.zeros((1, LINE), FLOAT)
    for place in range(8):
        ref, at, columns = joined_pieces(refs[:3])[place]
        matrix = ref[:, at : at + columns]
        total = jnp.sum(jnp.sum(matrix * matrix, axis=0, keepdims=True), axis=1, keepdims=True)
        totals = jnp.where(lane == place, total, totals)
    refs[3][...] = totals


def whole_call(kernel, shapes, *operands, places=0):
    memory = [pl.BlockSpec(memory_space=pltpu.SMEM)] * places
    memory += [pl.BlockSpec(memory_space=pltpu.VMEM)] * (len(operands) - places)
    return pl.pallas_call(
        kernel,
        in_specs=memory,
        out_specs=[pl.BlockSpec(memory_space=pltpu.VMEM)] * len(shapes),
        out_shape=[jax.ShapeDtypeStruct(shape, FLOAT) for shape in shapes],
        compiler_params=room(48),
        cost_estimate=LIGHT,
    )(*operands)


GELU_WIDTH = 0.7978845608028654
GELU_CUBE = 0.044715


def gelu_parts(values):
    square = values * values
    bend = jnp.tanh(values * (GELU_WIDTH + GELU_WIDTH * GELU_CUBE * square))
    half = 0.5 + 0.5 * bend
    slope = GELU_WIDTH + 3.0 * GELU_WIDTH * GELU_CUBE * square
    return values * half, half + (0.5 * values) * (1.0 - bend * bend) * slope


ROWS = 512
SHIFT_SELF, SCALE_SELF, GATE_SELF, SHIFT_MLP, SCALE_MLP, GATE_MLP = range(6)


def block_of(modulation_ref, place):
    return modulation_ref[:, place * D : (place + 1) * D]


def over_rows(frames, body, start=None):
    def step(place, carry):
        return body(pl.ds(pl.multiple_of(place * ROWS, ROWS), ROWS), carry)

    return lax.fori_loop(0, frames // ROWS, step, start)


def normed(values):
    centered = values - jnp.mean(values, axis=-1, keepdims=True)
    rate = lax.rsqrt(jnp.mean(centered * centered, axis=-1, keepdims=True) + EPS_NORM)
    return centered * rate, rate


def normed_back(grad, norm, rate):
    inner = jnp.mean(grad * norm, axis=-1, keepdims=True)
    return rate * (grad - jnp.mean(grad, axis=-1, keepdims=True) - norm * inner)


def down(values):
    return jnp.sum(values, axis=0, keepdims=True)


def no_sums(count):
    return (jnp.zeros((1, D), FLOAT),) * count


def first_kernel(
    in_ref, modulation_ref, query_weight_ref, pair_weight_ref, self_input_ref, query_ref, pair_ref
):
    shift = block_of(modulation_ref, SHIFT_SELF)
    scale = 1.0 + block_of(modulation_ref, SCALE_SELF)

    def some(rows, carry):
        norm, _ = normed(in_ref[rows, :].astype(FLOAT))
        self_input_ref[rows, :] = (norm * scale + shift).astype(BFLOAT)
        return carry

    over_rows(in_ref.shape[0], some)
    pair_ref[...] = nn(self_input_ref[...], pair_weight_ref[...]).astype(BFLOAT)
    query_ref[...] = nn(self_input_ref[...], query_weight_ref[...]).astype(BFLOAT)


def between_kernel(
    attn_ref,
    project_ref,
    in_ref,
    modulation_ref,
    query_weight_ref,
    branch_ref,
    after_ref,
    cross_input_ref,
    query_ref,
):
    branch_ref[...] = nn(attn_ref[...], project_ref[...])
    gate = block_of(modulation_ref, GATE_SELF)

    def some(rows, carry):
        after = in_ref[rows, :].astype(FLOAT) + gate * branch_ref[rows, :]
        after_ref[rows, :] = after
        norm, _ = normed(after)
        cross_input_ref[rows, :] = norm.astype(BFLOAT)
        return carry

    over_rows(in_ref.shape[0], some)
    query_ref[...] = nn(cross_input_ref[...], query_weight_ref[...]).astype(BFLOAT)


def mlp_kernel(
    attn_ref,
    project_ref,
    after_ref,
    modulation_ref,
    out_grad_ref,
    fc1_ref,
    fc2_ref,
    out_ref,
    res_grad_ref,
    cross_out_grad_ref,
    attn_grad_ref,
    sums_ref,
    part_ref,
    input_ref,
    grad_ref,
    input_t,
    grad_t,
    joined_ref,
    branch_ref,
    in_grad_ref,
):
    step = pl.program_id(0) * pl.num_programs(1) + pl.program_id(1)
    last = pl.num_programs(0) * pl.num_programs(1) - 1
    frames = attn_ref.shape[0]
    gate = block_of(modulation_ref, GATE_MLP)
    scale = 1.0 + block_of(modulation_ref, SCALE_MLP)

    @pl.when(step == 0)
    def _():
        shift = block_of(modulation_ref, SHIFT_MLP)
        joined_ref[...] = after_ref[...] + nn(attn_ref[...], project_ref[...])

        def some(rows, carry):
            norm, _ = normed(joined_ref[rows, :])
            input_ref[rows, :] = (norm * scale + shift).astype(BFLOAT)
            grad_ref[rows, :] = (gate * out_grad_ref[rows, :].astype(FLOAT)).astype(BFLOAT)
            return carry

        over_rows(frames, some)
        input_t[...] = input_ref[...].T
        grad_t[...] = grad_ref[...].T

    fc1, fc2 = fc1_ref[0], fc2_ref[0]
    act, slope = gelu_parts(nn(input_ref[...], fc1))
    act = act.astype(BFLOAT)
    pre_grad = (nn(grad_ref[...], fc2) * slope).astype(BFLOAT)
    branch, in_grad = nt(act, fc2), nt(pre_grad, fc1)

    @pl.when(step == 0)
    def _():
        branch_ref[...] = branch
        in_grad_ref[...] = in_grad

    @pl.when(step > 0)
    def _():
        branch_ref[...] += branch
        in_grad_ref[...] += in_grad

    far, size = part_ref.shape[2], part_ref.shape[4]
    for kind, product in enumerate((nn(input_t[...], pre_grad), nn(grad_t[...], act))):
        product = product.astype(BFLOAT)
        for place in range(4 * far):
            part_ref[0, place % 4, place // 4, kind] = product[place * size : (place + 1) * size]

    @pl.when(step == last)
    def _():
        def some(rows, carry):
            gate_sum, shift_sum, scale_sum = carry
            joined, branch_here = joined_ref[rows, :], branch_ref[rows, :]
            out_grad, in_grad_here = out_grad_ref[rows, :].astype(FLOAT), in_grad_ref[rows, :]
            out_ref[rows, :] = (joined + gate * branch_here).astype(BFLOAT)
            norm, rate = normed(joined)
            res_grad = out_grad + normed_back(in_grad_here * scale, norm, rate)
            res_grad_ref[rows, :] = res_grad
            cross_out_grad_ref[rows, :] = res_grad.astype(BFLOAT)
            return (
                gate_sum + down(out_grad * branch_here),
                shift_sum + down(in_grad_here),
                scale_sum + down(in_grad_here * norm),
            )

        gate_sum, shift_sum, scale_sum = over_rows(frames, some, no_sums(3))
        sums_ref[:, :D] = shift_sum
        sums_ref[:, D : 2 * D] = scale_sum
        sums_ref[:, 2 * D :] = gate_sum
        attn_grad_ref[...] = nt(cross_out_grad_ref[...], project_ref[...]).astype(BFLOAT)


def between_back_kernel(
    query_grad_ref,
    query_weight_ref,
    after_ref,
    res_grad_ref,
    branch_ref,
    modulation_ref,
    project_ref,
    self_res_ref,
    out_grad_ref,
    attn_grad_ref,
    sums_ref,
    in_grad_ref,
):
    in_grad_ref[...] = nt(query_grad_ref[...], query_weight_ref[...])
    gate = block_of(modulation_ref, GATE_SELF)

    def some(rows, carry):
        norm, rate = normed(after_ref[rows, :])
        res_grad = res_grad_ref[rows, :] + normed_back(in_grad_ref[rows, :], norm, rate)
        self_res_ref[rows, :] = res_grad
        out_grad_ref[rows, :] = (gate * res_grad).astype(BFLOAT)
        return (carry[0] + down(res_grad * branch_ref[rows, :]),)

    (sums_ref[...],) = over_rows(after_ref.shape[0], some, no_sums(1))
    attn_grad_ref[...] = nt(out_grad_ref[...], project_ref[...]).astype(BFLOAT)


def first_back_kernel(
    query_grad_ref,
    pair_grad_ref,
    query_weight_ref,
    pair_weight_ref,
    in_ref,
    modulation_ref,
    self_res_ref,
    out_ref,
    sums_ref,
    in_grad_ref,
):
    in_grad_ref[...] = nt(query_grad_ref[...], query_weight_ref[...]) + nt(
        pair_grad_ref[...], pair_weight_ref[...]
    )
    scale = 1.0 + block_of(modulation_ref, SCALE_SELF)

    def some(rows, carry):
        norm, rate = normed(in_ref[rows, :].astype(FLOAT))
        grad = in_grad_ref[rows, :]
        res_grad = self_res_ref[rows, :] + normed_back(grad * scale, norm, rate)
        out_ref[rows, :] = res_grad.astype(BFLOAT)
        return carry[0] + down(grad), carry[1] + down(grad * norm)

    shift_sum, scale_sum = over_rows(in_ref.shape[0], some, no_sums(2))
    sums_ref[:, :D] = shift_sum
    sums_ref[:, D:] = scale_sum


def left_half(weights):
    return weights, pl.BlockSpec((D, D), lambda step: (0, 0))


def right_half(weights):
    return weights, pl.BlockSpec((D, D), lambda step: (0, 1))


def frame_call(kernel, results, *operands, scratch=()):
    specs, arrays = [], []
    for operand in operands:
        if isinstance(operand, tuple):
            arrays.append(operand[0])
            specs.append(operand[1])
        else:
            arrays.append(operand)
            specs.append(whole_block(operand.shape))
    return pl.pallas_call(
        kernel,
        grid=(1,),
        in_specs=specs,
        out_specs=[whole_block(shape) for shape, _ in results],
        out_shape=[jax.ShapeDtypeStruct(shape, kind) for shape, kind in results],
        scratch_shapes=[pltpu.VMEM(shape, kind) for shape, kind in scratch],
        compiler_params=room(48),
        cost_estimate=LIGHT,
    )(*arrays)


MLP_TILE = 768


def mlp_both(cross_attn, project, after_self, modulation, out_grad, weights):
    frames = cross_attn.shape[0]
    far = lax.axis_size("far")
    rows = D // (4 * far)
    tiles = HALF // MLP_TILE
    once = dict(pipeline_mode=pl.Buffered(1))
    whole = pl.BlockSpec((frames, D), lambda half, tile: (0, 0), **once)
    square = (frames, D)
    return pl.pallas_call(
        mlp_kernel,
        grid=(2, tiles),
        in_specs=[
            whole,
            pl.BlockSpec((D, D), lambda half, tile: (0, 1), **once),
            whole,
            pl.BlockSpec((1, 6 * D), lambda half, tile: (0, 0)),
            whole,
            pl.BlockSpec((1, D, MLP_TILE), lambda half, tile: (half, 0, tile)),
            pl.BlockSpec((1, D, MLP_TILE), lambda half, tile: (half, 0, tile + tiles)),
        ],
        out_specs=[whole] * 4
        + [
            pl.BlockSpec((1, 3 * D), lambda half, tile: (0, 0)),
            pl.BlockSpec(
                (1, 4, far, 2, rows, MLP_TILE), lambda half, tile: (half, 0, 0, 0, 0, tile)
            ),
        ],
        out_shape=[
            jax.ShapeDtypeStruct(square, BFLOAT),
            jax.ShapeDtypeStruct(square, FLOAT),
            jax.ShapeDtypeStruct(square, BFLOAT),
            jax.ShapeDtypeStruct(square, BFLOAT),
            jax.ShapeDtypeStruct((1, 3 * D), FLOAT),
            jax.ShapeDtypeStruct((2, 4, far, 2, rows, HALF), BFLOAT),
        ],
        scratch_shapes=[
            pltpu.VMEM(square, BFLOAT),
            pltpu.VMEM(square, BFLOAT),
            pltpu.VMEM((D, frames), BFLOAT),
            pltpu.VMEM((D, frames), BFLOAT),
            pltpu.VMEM(square, FLOAT),
            pltpu.VMEM(square, FLOAT),
            pltpu.VMEM(square, FLOAT),
        ],
        compiler_params=room(48),
        cost_estimate=LIGHT,
    )(cross_attn, project, after_self, modulation, out_grad, weights, weights)


def per_device(
    block_in,
    text,
    timesteps,
    frame_mask,
    text_mask,
    cotangent,
    w_ada,
    w_qkv,
    w_out,
    w_cq,
    w_cout,
    w_ckv,
    w_fc1,
    w_fc2,
    row_state,
    col_state,
):
    clips = lax.axis_size(DP)
    devices = clips * 2
    data_at = lax.axis_index(DP)
    head_at = lax.axis_index("head")
    flat_at = data_at * 2 + head_at
    frames = block_in.shape[1]
    rows = w_qkv.shape[0]

    far = far_links()
    x_first = [far[0], row_link(), core_link()]
    y_first = [row_link(), far[0], core_link()]
    first = [
        gather_chain(
            with_bits(
                jnp.concatenate([w_qkv[:, :D], w_out, w_qkv[:, D:]], axis=1).astype(BFLOAT), "last"
            ),
            "last",
            far[:0:-1],
        )
    ]
    second = [
        gather_chain(
            with_bits(jnp.concatenate([w_cq, w_cout], axis=1).astype(BFLOAT), "last"),
            "last",
            far[:0:-1] + x_first,
        ),
        gather_chain(
            with_bits(w_ckv.astype(BFLOAT).reshape(w_ckv.shape[0], D), "columns"),
            "columns",
            far[:0:-1] + y_first,
        ),
    ]
    mlp_shard = jnp.concatenate([w_fc1.astype(BFLOAT), w_fc2.T.astype(BFLOAT)], axis=1)
    inputs = swap_place(block_in[0])
    joint_mask = jnp.concatenate([frame_mask[0], text_mask[0]])

    def add_step(link):
        return lambda state: state + cross(state, link)

    def project(steps):
        condition = embed_part(steps, flat_at * rows, rows)
        product = jnp.dot(condition, w_ada.astype(BFLOAT), preferred_element_type=FLOAT)
        return condition, product.reshape(clips // 2, 2, 6 * D)

    def keep_step(link):
        def step(state):
            condition, product = state
            bit = bit_of(link)
            dim = 1 if link == row_link() else dp_bits() - link[1].bit_length()
            kept = lax.dynamic_slice_in_dim(product, bit, 1, axis=dim)
            sent = lax.dynamic_slice_in_dim(product, 1 - bit, 1, axis=dim)
            product = kept + cross(sent, link)
            if link == row_link():
                product = product.reshape((2,) * (dp_bits() - 1) + (6 * D,))
            return condition, product

        return step

    def last_step(state):
        condition, product = state
        return condition, (product + cross(product, core_link())).reshape(1, 6 * D)

    steps = lax.dynamic_update_slice(jnp.zeros((clips,), jnp.int32), timesteps, (data_at,))
    timing = Chain(
        steps,
        [add_step(link) for link in [core_link()] + far_links()[1:] + far_links()[:1]]
        + [lambda steps: keep_step(row_link())(project(steps))]
        + [keep_step(link) for link in far_links()[1:] + far_links()[:1]]
        + [last_step],
    )
    far_count = len(far) - 1
    slots = far_count + 3
    for slot in range(slots):
        if slot < far_count:
            timing.advance(1 + (slot == 0) + (slot == far_count - 1))
        else:
            timing.advance((1, far_count, 2)[slot - far_count])
        if slot == far_count:
            joint = first[0].state
            first = [
                gather_chain(joint[..., : 2 * D], "last", x_first),
                gather_chain(joint[..., 2 * D :], "last", y_first),
            ]
        for chain in first:
            chain.advance()
        if slot >= 2:
            for chain in second:
                chain.advance()
        if slot == far_count - 1:
            inputs, mlp_shard, joint_mask, text = tie(
                [timing] + first + second, inputs, mlp_shard, joint_mask, text
            )
            mlp_all = lax.all_gather(mlp_shard, HEAD + DP, axis=0, tiled=True)
            masks = from_clip_core(joint_mask)
            clip_text = from_clip_core(text[0])
        elif slot < slots - 1:
            tie([timing] + first + (second if slot == far_count else []))
        else:
            wide = tie([timing] + first, w_ada, w_qkv, w_out, w_cq, w_cout, w_fc1, w_fc2)
            masters = [
                jnp.concatenate(wide[:5], axis=1),
                w_ckv.reshape(w_ckv.shape[0], D),
                jnp.concatenate([wide[5], wide[6].T], axis=1),
            ]
            (weight_squares,) = whole_call(weight_kernel, [(1, LINE)], *masters)
    condition, modulation = timing.finish()
    query_out, w_key_value = [chain.finish().reshape(D, 2 * D) for chain in first]
    square = (frames, D)
    core_at = data_at % 2
    own_allowed = lax.dynamic_slice_in_dim(masks, core_at * frames, frames)
    other_allowed = lax.dynamic_slice_in_dim(masks, (1 - core_at) * frames, frames)
    own_bias, other_bias = bias_of(own_allowed), bias_of(other_allowed)
    text_bias = bias_of(masks[2 * frames :])

    self_input, query, key_value = frame_call(
        first_kernel,
        [(square, BFLOAT), (square, BFLOAT), ((frames, 2 * D), BFLOAT)],
        inputs,
        modulation,
        left_half(query_out),
        w_key_value,
    )
    other_key_value = cross(key_value, core_link())
    query, other_key_value = tie(second, query, other_key_value)
    for chain in second:
        chain.advance()

    self_keys = [(key_value, own_bias), (other_key_value, other_bias)]
    self_attn, self_logs = attend(query, self_keys, plain_places, 2)
    self_attn, cotangent = tie(second, self_attn, cotangent)
    swapped_cotangent = swap_only(cotangent[0])
    cross_pair, w_text = [chain.finish() for chain in second]
    cross_pair, w_text = cross_pair.reshape(D, 2 * D), w_text.reshape(DT, 2 * D)
    self_branch, after_self, cross_input, cross_query = frame_call(
        between_kernel,
        [(square, FLOAT), (square, FLOAT), (square, BFLOAT), (square, BFLOAT)],
        self_attn,
        right_half(query_out),
        inputs,
        modulation,
        left_half(cross_pair),
    )

    text_pair = nn(clip_text, w_text).astype(BFLOAT)
    text_keys = [(text_pair, text_bias)]
    cross_attn, cross_logs = attend(cross_query, text_keys, half_places, PAIRS // 2)

    cross_attn, own, cotangent = tie([], cross_attn, on_own_chip(), cotangent)
    out_grad = jnp.where(own, cotangent[0], swapped_cotangent)
    block_out, cross_res_grad, cross_out_grad, cross_attn_grad, mlp_sums, mlp_part = mlp_both(
        cross_attn,
        cross_pair,
        after_self,
        modulation,
        out_grad,
        mlp_all.reshape(2, D, 2 * HALF),
    )
    mlp_part = lax.psum_scatter(
        mlp_part.reshape((8,) + mlp_part.shape[2:]),
        HEAD + ("near", "core"),
        scatter_dimension=0,
        tiled=False,
    )

    cross_query_grad, text_pair_grad = attend_back(
        cross_query, cross_attn, cross_attn_grad, cross_logs, text_keys, half_places, PAIRS // 2
    )
    self_res_grad, self_out_grad, self_attn_grad, gate_self_grad = frame_call(
        between_back_kernel,
        [(square, FLOAT), (square, BFLOAT), (square, BFLOAT), ((1, D), FLOAT)],
        cross_query_grad,
        left_half(cross_pair),
        after_self,
        cross_res_grad,
        self_branch,
        modulation,
        right_half(query_out),
        scratch=[(square, FLOAT)],
    )

    query_grad, own_pair_grad, other_pair_grad = attend_back(
        query, self_attn, self_attn_grad, self_logs, self_keys, plain_places, 2
    )
    pair_grad = (
        own_pair_grad.astype(FLOAT) + cross(other_pair_grad, core_link()).astype(FLOAT)
    ).astype(BFLOAT)
    last_chains = [
        scatter_chain(
            outer((self_input, query_grad), (self_attn, self_out_grad)), "last", False
        ),
        scatter_chain(outer((self_input, pair_grad)), "last", True),
    ]
    cross_query_grad, text_pair_grad = tie(last_chains, cross_query_grad, text_pair_grad)
    for chain in last_chains:
        chain.advance()
    cross_chains = [
        scatter_chain(
            outer((cross_input, cross_query_grad), (cross_attn, cross_out_grad)), "last", False
        ),
        scatter_chain(outer((clip_text, text_pair_grad)), "columns", True),
    ]
    query_grad, pair_grad = tie(cross_chains + last_chains, query_grad, pair_grad)
    for chain in last_chains + cross_chains:
        chain.advance()
    input_grad, self_sums = frame_call(
        first_back_kernel,
        [(square, BFLOAT), ((1, 2 * D), FLOAT)],
        query_grad,
        pair_grad,
        left_half(query_out),
        w_key_value,
        inputs,
        modulation,
        self_res_grad,
        scratch=[(square, FLOAT)],
    )
    modulation_grad = jnp.concatenate([self_sums, gate_self_grad, mlp_sums], axis=-1)

    def join_step(link):
        def step(state):
            other = cross(state, link)
            upper = bit_of(link) == 1
            dim = dp_bits() - 1 if link[0] == HEAD else dp_bits() - link[1].bit_length()
            low, high = jnp.where(upper, other, state), jnp.where(upper, state, other)
            return jnp.concatenate([low, high], axis=dim)

        return step

    far = far_links()
    shape = (1,) * dp_bits() + (6 * D,)
    joining = Chain(
        modulation_grad,
        [lambda state: (state + cross(state, core_link())).reshape(shape)]
        + [join_step(link) for link in far[:0:-1] + [far[0], row_link()]],
    )

    chains = last_chains + cross_chains
    joining.advance()
    block_out, input_grad, mlp_part = tie([joining] + chains, block_out, input_grad, mlp_part)
    mlp_raw = lax.psum_scatter(mlp_part, "far", scatter_dimension=0, tiled=False).astype(FLOAT)
    for chain in chains:
        chain.advance()
    joining.advance(len(far) - 1)
    block_out, input_grad = tie([joining] + chains, block_out, input_grad)
    for chain in chains:
        chain.advance()
    joining.advance(2)
    block_out, input_grad, mlp_raw = tie([joining] + chains, block_out, input_grad, mlp_raw)
    for chain in chains:
        chain.advance()
    block_out, input_grad = tie(chains, block_out, input_grad)
    other_out, other_grad = swap_only(block_out), swap_only(input_grad)
    for chain in cross_chains:
        chain.advance()
    tie(cross_chains)
    modulation_grad = joining.finish()
    ada_raw = jnp.einsum(
        "cr,cx->rx",
        condition.astype(FLOAT),
        modulation_grad.reshape(clips, 6 * D),
        precision=PRECISE,
    )

    cross_raw, ckv_raw = [chain.finish() for chain in cross_chains]
    query_out_raw, pair_raw = [chain.finish() for chain in last_chains]

    place = jnp.stack([data_at, head_at]).astype(jnp.int32)
    raw_grads = [ada_raw, query_out_raw, pair_raw, cross_raw, ckv_raw, mlp_raw]
    (statistics,) = whole_call(
        statistics_kernel, [(STAT_LINES, LINE)], place, weight_squares, *raw_grads, places=1
    )
    sums = sum_all(statistics)
    shapes = [(rows, columns) for columns in COL_SIZES[:5]]
    shapes += [masters[1].shape] + [(rows * 2, HALF)] * 2
    line = (1, LINE)
    row_new, col_new, norm, update_squares, *rest = whole_call(
        update_kernel,
        [(ROW_LINES, LINE), (COL_LINES, LINE), line, line]
        + shapes
        + [master.shape for master in masters],
        place,
        sums,
        row_state.reshape(ROW_LINES, LINE),
        col_state.reshape(COL_LINES, LINE),
        *raw_grads,
        places=1,
    )
    clipped, updates = list(rest[:8]), rest[8:]
    clipped[5] = clipped[5].reshape(w_ckv.shape)
    clipped[7] = clipped[7].T
    late, _ = tie([], on_own_chip(), update_squares)
    block_out = jnp.where(late, block_out, other_out)
    input_grad = jnp.where(late, input_grad, other_grad)
    update_squares, block_out, input_grad, *clipped = tie(
        [], sum_all(update_squares), block_out, input_grad, *clipped
    )
    updated = list(
        whole_call(
            apply_kernel,
            shapes,
            update_squares,
            sums[STAT_LINES - 2 : STAT_LINES - 1],
            *masters,
            *updates,
        )
    )
    updated[5] = updated[5].reshape(w_ckv.shape)
    updated[7] = updated[7].T
    return (
        block_out[None],
        input_grad[None],
        norm[0, 0],
        row_new.reshape(-1),
        col_new.reshape(-1),
        *clipped,
        *updated,
    )


def solution(mesh):
    devices = mesh.devices
    refined = jax.sharding.Mesh(devices.reshape(devices.shape[0] // 4, 2, 2, 2), ALL)
    return jax.shard_map(
        per_device,
        mesh=refined,
        in_specs=(
            P(DP, "head", None),
            P(DP, None, None),
            P(DP),
            P(DP, None),
            P(DP, None),
            P(DP, "head", None),
            P(ALL, None),
            P(ALL, None),
            P(ALL, None),
            P(ALL, None),
            P(ALL, None),
            P(DP, None, "head"),
            P(DP, "head"),
            P("head", DP),
            P(),
            P(),
        ),
        out_specs=(
            P(DP, "head", None),
            P(DP, "head", None),
            P(),
            P(),
            P(),
            P(ALL, None),
            P(ALL, None),
            P(ALL, None),
            P(ALL, None),
            P(ALL, None),
            P(DP, None, "head"),
            P(DP, "head"),
            P("head", DP),
            P(ALL, None),
            P(ALL, None),
            P(ALL, None),
            P(ALL, None),
            P(ALL, None),
            P(DP, None, "head"),
            P(DP, "head"),
            P("head", DP),
        ),
        check_vma=False,
    )
```

profile of v0, /device:TPU:0, one launch (start us, length us, event | category | flops | bytes accessed | tf_op | source)
XLA Modules:
  0.0 406.2 jit_solution(16548398441418462645)
XLA Ops:
  9.2 4.1 %collective-permute-start.2 = (bf16[1,1,1,1,1,24,3072]{6,5,4,3,2,1,0:T(8,128)(2,1)S(1)}, bf16[1,1,1,1,1,24,3072]{6,5,4,3,2,1,0:T(8,128)(2,1)S(1)}, u32[]{:S(2)}, u32[]{:S(2)}) collective-permute-start(bf16[1,1,1,1,1,24,3072]{6,5,4,3,2,1,0:T(8,128)(2,1)S(1)} %pad_maximum_fusion.20), channel_id=1, source_target_pairs={{0,16},{2,18},{4,20},{6,22},{8,24},{10,26},{12,28},{14,30},{16,0},... | collective-permute-start | bytes 442376 | tf_op jit(solution)/shard_map/ppermute | solution.py:70
  19.8 2.0 collective-permute-done.1
  25.4 5.5 %collective-permute-done.3 = s32[16]{0:T(128)S(1)} collective-permute-done((s32[16]{0:T(128)S(1)}, s32[16]{0:T(128)S(1)}, u32[]{:S(2)}, u32[]{:S(2)}) %collective-permute-start.3) | collective-permute-done | bytes 96 | tf_op jit(solution)/shard_map/ppermute | solution.py:70
  32.3 2.0 collective-permute-done.4
  34.6 3.4 collective-permute-start.11
  45.8 6.1 %collective-permute-done.7 = f32[8,1,4608]{2,1,0:T(1,128)S(1)} collective-permute-done((f32[8,1,4608]{2,1,0:T(1,128)S(1)}, f32[8,1,4608]{2,1,0:T(1,128)S(1)}, u32[]{:S(2)}, u32[]{:S(2)}) %collective-permute-start.7) | collective-permute-done | bytes 147488 | tf_op jit(solution)/shard_map/ppermute | solution.py:70
  53.9 4.5 %collective-permute-done.12 = f32[2,1,2,4608]{3,2,1,0:T(2,128)S(1)} collective-permute-done((f32[2,1,2,4608]{3,2,1,0:T(2,128)S(1)}, f32[2,1,2,4608]{3,2,1,0:T(2,128)S(1)}, u32[]{:S(2)}, u32[]{:S(2)}) %collective-permute-start.12) | collective-permute-done | bytes 73760 | tf_op jit(solution)/shard_map/ppermute | solution.py:70
  58.5 2.8 collective-permute-start.13
  65.0 8.8 %collective-permute-done.15 = bf16[2,2,1,1,2,24,1536]{6,5,4,3,2,1,0:T(8,128)(2,1)S(1)} collective-permute-done((bf16[2,2,1,1,2,24,1536]{6,5,4,3,2,1,0:T(8,128)(2,1)S(1)}, bf16[2,2,1,1,2,24,1536]{6,5,4,3,2,1,0:T(8,128)(2,1)S(1)}, u32[]{:S(2)}, u32[]{:S(2)}) %collective-permute-start.15) | collective-permute-done | bytes 589856 | tf_op jit(solution)/shard_map/ppermute | solution.py:70
  75.9 2.6 collective-permute-done.16
  84.8 4.4 %shard_map.320 = (bf16[512,768]{1,0:T(8,128)(2,1)S(1)}, bf16[512,768]{1,0:T(8,128)(2,1)S(1)}, bf16[512,1536]{1,0:T(8,128)(2,1)S(1)}) custom-call(bf16[512,768]{1,0:T(8,128)(2,1)S(1)} %broadcast_select_fusion.12.in_ref, f32[1,4608]{1,0:T(1,128)S(1)} %add_bitcast_fusion.1.modulation_ref, bf16[768,1536]{1,0:T(8,128)(2,1)} %bitcast.82, bf16[768,1536]{1,0:T(8,128)(2,1)} %bitcast.91), custom_call_target="tpu_custom_call" | custom-call | flops 1000 | bytes 1000 | tf_op jit(solution)/shard_map/pallas_call | solution.py:841
  91.2 9.9 %collective-permute-done.23 = bf16[2,2,1,1,64,768]{5,4,3,2,1,0:T(8,128)(2,1)S(1)} collective-permute-done((bf16[2,2,1,1,64,768]{5,4,3,2,1,0:T(8,128)(2,1)S(1)}, bf16[2,2,1,1,64,768]{5,4,3,2,1,0:T(8,128)(2,1)S(1)}, u32[]{:S(2)}, u32[]{:S(2)}) %collective-permute-start.23) | collective-permute-done | bytes 393248 | tf_op jit(solution)/shard_map/ppermute | solution.py:70
  106.8 11.3 %shard_map.321 = (bf16[512,768]{1,0:T(8,128)(2,1)S(1)}, f32[6,2,512]{2,1,0:T(2,128)S(1)}) custom-call(bf16[512,768]{1,0:T(8,128)(2,1)S(1)} %copy-done.14, bf16[512,1536]{1,0:T(8,128)(2,1)S(1)} %get-tuple-element.196.refs_1_.refs_2_.refs_4_.refs_5_, bf16[512,1536]{1,0:T(8,128)(2,1)S(1)} %get-tuple-element.196.refs_1_.refs_2_.refs_4_.refs_5_, ...), custom_call_target="tpu_custom_call" | custom-call | flops 1000 | bytes 1000 | tf_op jit(solution)/shard_map/pallas_call | solution.py:322
  118.0 12.7 %collective-permute-done.25 = bf16[2,2,2,1,1,24,1536]{6,5,4,3,2,1,0:T(8,128)(2,1)} collective-permute-done((bf16[2,2,2,1,1,24,1536]{6,5,4,3,2,1,0:T(8,128)(2,1)}, bf16[2,2,2,1,1,24,1536]{6,5,4,3,2,1,0:T(8,128)(2,1)}, u32[]{:S(2)}, u32[]{:S(2)}) %collective-permute-start.25) | collective-permute-done | bytes 589856 | tf_op jit(solution)/shard_map/ppermute | solution.py:70
  132.2 2.8 collective-permute-done.26
  136.2 2.0 collective-permute-start.29
  138.3 2.1 collective-permute-done.29
  143.0 3.9 shard_map.322
  149.8 4.8 %shard_map.323 = (bf16[512,768]{1,0:T(8,128)(2,1)S(1)}, f32[6,2,512]{2,1,0:T(2,128)S(1)}) custom-call(bf16[512,768]{1,0:T(8,128)(2,1)S(1)} %get-tuple-element.207.refs_0_, bf16[256,1536]{1,0:T(8,128)(2,1)S(1)} %convolution_convert_fusion.refs_1_.refs_2_.refs_4_.refs_5_, bf16[256,1536]{1,0:T(8,128)(2,1)S(1)} %convolution_convert_fusion.refs_1_.refs_2_.refs_4_.refs_5_, ...), custom_call_target="tpu_custom_call" | custom-call | flops 1000 | bytes 1000 | tf_op jit(solution)/shard_map/pallas_call | solution.py:322
  154.8 25.0 %shard_map.324 = (bf16[512,768]{1,0:T(8,128)(2,1)S(1)}, f32[512,768]{1,0:T(8,128)S(1)}, bf16[512,768]{1,0:T(8,128)(2,1)S(1)}, bf16[512,768]{1,0:T(8,128)(2,1)S(1...) custom-call(bf16[512,768]{1,0:T(8,128)(2,1)S(1)} %get-tuple-element.212.attn_ref.refs_1_.refs_2_, ...), custom_call_target="tpu_custom_call" | custom-call | flops 1000 | bytes 1000 | tf_op jit(solution)/shard_map/pallas_call | solution.py:864
  186.0 6.8 %shard_map.325 = (bf16[512,768]{1,0:T(8,128)(2,1)S(1)}, bf16[256,1536]{1,0:T(8,128)(2,1)S(1)}) custom-call(bf16[512,768]{1,0:T(8,128)(2,1)S(1)} %copy-done.21, bf16[512,768]{1,0:T(8,128)(2,1)S(1)} %get-tuple-element.212.attn_ref.refs_1_.refs_2_, bf16[512,768]{1,0:T(8,128)(2,1)S(1)} %copy-done.42, f32[6,2,512]{2,1,0:T(2,128)S(1)} %get-tuple-element.218.refs_3_, ...), custom_call_target="tpu_custom_call" | custom-call | flops 1000 | bytes 1000 | tf_op jit(solution)/shard_map/pallas_call | solution.py:339
  193.7 6.5 %shard_map.326 = (f32[512,768]{1,0:T(8,128)S(1)}, bf16[512,768]{1,0:T(8,128)(2,1)S(1)}, bf16[512,768]{1,0:T(8,128)(2,1)S(1)}, f32[1,768]{1,0:T(1,128)S(1)}) custom-call(bf16[512,768]{1,0:T(8,128)(2,1)S(1)} %get-tuple-element.229.query_grad_ref.refs_1_, bf16[768,1536]{1,0:T(8,128)(2,1)} %bitcast.88, f32[512,768]{1,0:T(8,128)S(1)} %copy-done.8, ...), custom_call_target="tpu_custom_call" | custom-call | flops 1000 | bytes 1000 | tf_op jit(solution)/shard_map/pallas_call | solution.py:841
  201.4 21.1 %shard_map.327 = (bf16[512,768]{1,0:T(8,128)(2,1)S(1)}, bf16[512,1536]{1,0:T(8,128)(2,1)S(1)}, bf16[512,1536]{1,0:T(8,128)(2,1)}) custom-call(bf16[512,768]{1,0:T(8,128)(2,1)S(1)} %copy-done.15, bf16[512,768]{1,0:T(8,128)(2,1)S(1)} %copy-done.7, bf16[512,768]{1,0:T(8,128)(2,1)S(1)} %get-tuple-element.222.refs_2_, ...), custom_call_target="tpu_custom_call" | custom-call | flops 1000 | bytes 1000 | tf_op jit(solution)/shard_map/pallas_call | solution.py:339
  223.6 2.3 collective-permute-start.32
  229.3 2.4 add_convert_fusion.1.refs_1_.pair_grad_ref
  244.7 2.0 add_convert_fusion.3
  252.0 4.7 %shard_map.332 = (bf16[512,768]{1,0:T(8,128)(2,1)S(1)}, f32[1,1536]{1,0:T(1,128)S(1)}) custom-call(bf16[512,768]{1,0:T(8,128)(2,1)S(1)} %copy-done.23, bf16[512,1536]{1,0:T(8,128)(2,1)S(1)} %add_convert_fusion.1.refs_1_.pair_grad_ref, bf16[768,1536]{1,0:T(8,128)(2,1)} %bitcast.85, bf16[768,1536]{1,0:T(8,128)(2,1)} %bitcast.92, ...), custom_call_target="tpu_custom_call" | custom-call | flops 1000 | bytes 1000 | tf_op jit(solution)/shard_map/pallas_call | solution.py:841
  258.0 14.8 %collective-permute-done.37 = bf16[2,2,1,1,2,24,1536]{6,5,4,3,2,1,0:T(8,128)(2,1)} collective-permute-done((bf16[2,2,1,1,2,24,1536]{6,5,4,3,2,1,0:T(8,128)(2,1)S(1)}, bf16[2,2,1,1,2,24,1536]{6,5,4,3,2,1,0:T(8,128)(2,1)}, u32[]{:S(2)}, u32[]{:S(2)}) %collective-permute-start.37) | collective-permute-done | bytes 589856 | tf_op jit(solution)/shard_map/ppermute | solution.py:70
  272.8 2.0 add_convert_fusion.7
  275.8 2.7 add_convert_fusion.2
  282.8 2.4 collective-permute-start.40
  291.7 11.4 %collective-permute-done.43 = bf16[2,2,1,1,1,24,1536]{6,5,4,3,2,1,0:T(8,128)(2,1)} collective-permute-done((bf16[2,2,1,1,1,24,1536]{6,5,4,3,2,1,0:T(8,128)(2,1)S(1)}, bf16[2,2,1,1,1,24,1536]{6,5,4,3,2,1,0:T(8,128)(2,1)}, u32[]{:S(2)}, u32[]{:S(2)}) %collective-permute-start.43) | collective-permute-done | bytes 294944 | tf_op jit(solution)/shard_map/ppermute | solution.py:70
  315.6 4.8 %collective-permute-done.46 = f32[2,2,1,1,4608]{4,3,2,1,0:T(1,128)S(1)} collective-permute-done((f32[2,2,1,1,4608]{4,3,2,1,0:T(1,128)S(1)}, f32[2,2,1,1,4608]{4,3,2,1,0:T(1,128)S(1)}, u32[]{:S(2)}, u32[]{:S(2)}) %collective-permute-start.46) | collective-permute-done | bytes 73760 | tf_op jit(solution)/shard_map/ppermute | solution.py:70
  323.1 2.7 collective-permute-done.47
  331.8 2.5 collective-permute-start.53
  334.8 1.9 reshape.232
  342.6 2.1 collective-permute-start.56
  348.8 3.0 collective-permute-done.57
  355.2 3.7 collective-permute-done.59
  360.2 3.4 collective-permute-done.60
  364.5 5.6 %collective-permute-done.61 = f32[184,128]{1,0:T(8,128)S(1)} collective-permute-done((f32[184,128]{1,0:T(8,128)S(1)}, f32[184,128]{1,0:T(8,128)S(1)}, u32[]{:S(2)}, u32[]{:S(2)}) %collective-permute-start.61) | collective-permute-done | bytes 94240 | tf_op jit(solution)/shard_map/ppermute | solution.py:70
  370.3 4.5 %collective-permute-done.62 = f32[184,128]{1,0:T(8,128)S(1)} collective-permute-done((f32[184,128]{1,0:T(8,128)S(1)}, f32[184,128]{1,0:T(8,128)S(1)}, u32[]{:S(2)}, u32[]{:S(2)}) %collective-permute-start.62) | collective-permute-done | bytes 94240 | tf_op jit(solution)/shard_map/ppermute | solution.py:70
  374.9 2.1 shard_map.334
  379.6 3.5 collective-permute-done.64
  383.3 3.3 collective-permute-done.65
  386.9 4.2 %collective-permute-done.66 = f32[1,128]{1,0:T(1,128)S(1)} collective-permute-done((f32[1,128]{1,0:T(1,128)S(1)}, f32[1,128]{1,0:T(1,128)S(1)}, u32[]{:S(2)}, u32[]{:S(2)}) %collective-permute-start.66) | collective-permute-done | bytes 544 | tf_op jit(solution)/shard_map/ppermute | solution.py:70
  391.2 1.7 reshape.239
  392.9 1.8 collective-permute-done.67
  (416 shorter events, 139.2 us)
Async XLA Ops:
  7.2 147.5 %all-gather.2.cloned.1.call-start = ((), (), s32[]{:S(2)}) async-start(), calls=%async_computation.2 | async-start | bytes 9732096 | tf_op jit(solution)/shard_map/all_gather | solution.py:1015
  9.2 12.5 %collective-permute-start.2 = (bf16[1,1,1,1,1,24,3072]{6,5,4,3,2,1,0:T(8,128)(2,1)S(1)}, bf16[1,1,1,1,1,24,3072]{6,5,4,3,2,1,0:T(8,128)(2,1)S(1)}, u32[]{:S(2)}, u32[]{:S(2)}) collective-permute-start(bf16[1,1,1,1,1,24,3072]{6,5,4,3,2,1,0:T(8,128)(2,1)S(1)} %pad_maximum_fusion.20), channel_id=1, source_target_pairs={{0,16},{2,18},{4,20},{6,22},{8,24},{10,26},{12,28},{14,30},{16,0},... | collective-permute-start | bytes 442376 | tf_op jit(solution)/shard_map/ppermute | solution.py:70
  14.1 20.4 %collective-permute-start.6 = (bf16[512,768]{1,0:T(8,128)(2,1)}, bf16[512,768]{1,0:T(8,128)(2,1)}, u32[]{:S(2)}, u32[]{:S(2)}) collective-permute-start(bf16[512,768]{1,0:T(8,128)(2,1)} %bitcast.97), channel_id=1, source_target_pairs={{1,2},{2,1},{5,6},{6,5},{9,10},{10,9},{13,14},{14,13},{17,18},{18,... | collective-permute-start | bytes 2359304 | tf_op jit(solution)/shard_map/ppermute | solution.py:159
  21.8 12.5 %collective-permute-start.5 = (bf16[2,1,1,1,1,24,3072]{6,5,4,3,2,1,0:T(8,128)(2,1)S(1)}, bf16[2,1,1,1,1,24,3072]{6,5,4,3,2,1,0:T(8,128)(2,1)S(1)}, u32[]{:S(2)}, u32[]{:S(2)}) collective-permute-start(bf16[2,1,1,1,1,24,3072]{6,5,4,3,2,1,0:T(8,128)(2,1)S(1)} %pad_maximum_fusion.15), channel_id=1, source_target_pairs={{0,8},{2,10},{4,12},{6,14},{8,0},{10,2},{12,4},{14,6},{16,24},{18,... | collective-permute-start | bytes 884744 | tf_op jit(solution)/shard_map/ppermute | solution.py:70
  24.2 6.6 %collective-permute-start.3 = (s32[16]{0:T(128)S(1)}, s32[16]{0:T(128)S(1)}, u32[]{:S(2)}, u32[]{:S(2)}) collective-permute-start(s32[16]{0:T(128)S(1)} %add.409), channel_id=1, source_target_pairs={{0,16},{2,18},{4,20},{6,22},{8,24},{10,26},{12,28},{14,30},{16,0},... | collective-permute-start | bytes 200 | tf_op jit(solution)/shard_map/ppermute | solution.py:70
  34.6 11.0 %collective-permute-start.11 = (bf16[1,1,1,1,64,768]{5,4,3,2,1,0:T(8,128)(2,1)S(1)}, bf16[1,1,1,1,64,768]{5,4,3,2,1,0:T(8,128)(2,1)S(1)}, u32[]{:S(2)}, u32[]{:S(2)}) collective-permute-start(bf16[1,1,1,1,64,768]{5,4,3,2,1,0:T(8,128)(2,1)S(1)} %reshape_reshape.3), channel_id=1, source_target_pairs={{0,16},{2,18},{4,20},{6,22},{8,24},{10,26},{12,28},{14,30},{16,0},... | collective-permute-start | bytes 294920 | tf_op jit(solution)/shard_map/ppermute | solution.py:70
  38.0 7.6 %collective-permute-start.10 = (bf16[1,1,1,1,1,24,1536]{6,5,4,3,2,1,0:T(8,128)(2,1)S(1)}, bf16[1,1,1,1,1,24,1536]{6,5,4,3,2,1,0:T(8,128)(2,1)S(1)}, u32[]{:S(2)}, u32[]{:S(2)}) collective-permute-start(bf16[1,1,1,1,1,24,1536]{6,5,4,3,2,1,0:T(8,128)(2,1)S(1)} %pad_maximum_fusion.23), channel_id=1, source_target_pairs={{0,16},{2,18},{4,20},{6,22},{8,24},{10,26},{12,28},{14,30},{16,0},... | collective-permute-start | bytes 221192 | tf_op jit(solution)/shard_map/ppermute | solution.py:70
  39.0 13.5 %collective-permute-start.8 = (bf16[2,2,1,1,1,24,1536]{6,5,4,3,2,1,0:T(8,128)(2,1)}, bf16[2,2,1,1,1,24,1536]{6,5,4,3,2,1,0:T(8,128)(2,1)S(1)}, u32[]{:S(2)}, u32[]{:S(2)}) collective-permute-start(bf16[2,2,1,1,1,24,1536]{6,5,4,3,2,1,0:T(8,128)(2,1)} %get-tuple-element.340), channel_id=1, source_target_pairs={{0,4},{2,6},{4,0},{6,2},{8,12},{10,14},{12,8},{14,10},{16,20},{18,... | collective-permute-start | bytes 884744 | tf_op jit(solution)/shard_map/ppermute | solution.py:70
  40.5 12.0 %collective-permute-start.9 = (bf16[2,2,1,1,1,24,1536]{6,5,4,3,2,1,0:T(8,128)(2,1)}, bf16[2,2,1,1,1,24,1536]{6,5,4,3,2,1,0:T(8,128)(2,1)}, u32[]{:S(2)}, u32[]{:S(2)}) collective-permute-start(bf16[2,2,1,1,1,24,1536]{6,5,4,3,2,1,0:T(8,128)(2,1)} %get-tuple-element.339), channel_id=1, source_target_pairs={{0,1},{1,0},{2,3},{3,2},{4,5},{5,4},{6,7},{7,6},{8,9},{9,8},{10,11... | collective-permute-start | bytes 884744 | tf_op jit(solution)/shard_map/ppermute | solution.py:70
  43.4 8.5 %collective-permute-start.7 = (f32[8,1,4608]{2,1,0:T(1,128)S(1)}, f32[8,1,4608]{2,1,0:T(1,128)S(1)}, u32[]{:S(2)}, u32[]{:S(2)}) collective-permute-start(f32[8,1,4608]{2,1,0:T(1,128)S(1)} %constant_dynamic-slice_fusion.23), channel_id=1, source_target_pairs={{0,1},{1,0},{2,3},{3,2},{4,5},{5,4},{6,7},{7,6},{8,9},{9,8},{10,11... | collective-permute-start | bytes 442376 | tf_op jit(solution)/shard_map/ppermute | solution.py:70
  43.9 235.0 %reduce-scatter.3.cloned.1.call-start = ((), (), s32[]{:S(2)}) async-start(), calls=%async_computation.3 | async-start | bytes 10616832 | tf_op jit(solution)/shard_map/reduce_scatter | solution.py:1080
  58.5 6.5 %collective-permute-start.13 = (f32[1,1,2,4608]{3,2,1,0:T(2,128)S(1)}, f32[1,1,2,4608]{3,2,1,0:T(2,128)S(1)}, u32[]{:S(2)}, u32[]{:S(2)}) collective-permute-start(f32[1,1,2,4608]{3,2,1,0:T(2,128)S(1)} %constant_dynamic-slice_fusion.21), channel_id=1, source_target_pairs={{0,16},{2,18},{4,20},{6,22},{8,24},{10,26},{12,28},{14,30},{16,0},... | collective-permute-start | bytes 110600 | tf_op jit(solution)/shard_map/ppermute | solution.py:70
  61.3 12.6 %collective-permute-start.15 = (bf16[2,2,1,1,2,24,1536]{6,5,4,3,2,1,0:T(8,128)(2,1)S(1)}, bf16[2,2,1,1,2,24,1536]{6,5,4,3,2,1,0:T(8,128)(2,1)S(1)}, u32[]{:S(2)}, u32[]{:S(2)}) collective-permute-start(bf16[2,2,1,1,2,24,1536]{6,5,4,3,2,1,0:T(8,128)(2,1)S(1)} %pad_maximum_fusion.11), channel_id=1, source_target_pairs={{0,4},{2,6},{4,0},{6,2},{8,12},{10,14},{12,8},{14,10},{16,20},{18,... | collective-permute-start | bytes 1769480 | tf_op jit(solution)/shard_map/ppermute | solution.py:70
  62.6 11.5 %collective-permute-start.14 = (bf16[2,2,2,1,1,24,1536]{6,5,4,3,2,1,0:T(8,128)(2,1)S(1)}, bf16[2,2,2,1,1,24,1536]{6,5,4,3,2,1,0:T(8,128)(2,1)S(1)}, u32[]{:S(2)}, u32[]{:S(2)}) collective-permute-start(bf16[2,2,2,1,1,24,1536]{6,5,4,3,2,1,0:T(8,128)(2,1)S(1)} %pad_maximum_fusion.10), channel_id=1, source_target_pairs={{0,1},{1,0},{2,3},{3,2},{4,5},{5,4},{6,7},{7,6},{8,9},{9,8},{10,11... | collective-permute-start | bytes 1769480 | tf_op jit(solution)/shard_map/ppermute | solution.py:70
  63.0 26.6 %collective-permute-start.22 = (bf16[2,1,1,1,64,768]{5,4,3,2,1,0:T(8,128)(2,1)S(1)}, bf16[2,1,1,1,64,768]{5,4,3,2,1,0:T(8,128)(2,1)S(1)}, u32[]{:S(2)}, u32[]{:S(2)}) collective-permute-start(bf16[2,1,1,1,64,768]{5,4,3,2,1,0:T(8,128)(2,1)S(1)} %pad_maximum_fusion.19), channel_id=1, source_target_pairs={{0,8},{2,10},{4,12},{6,14},{8,0},{10,2},{12,4},{14,6},{16,24},{18,... | collective-permute-start | bytes 589832 | tf_op jit(solution)/shard_map/ppermute | solution.py:70
  64.0 11.8 %collective-permute-start.20 = (bf16[2,1,1,1,1,24,1536]{6,5,4,3,2,1,0:T(8,128)(2,1)S(1)}, bf16[2,1,1,1,1,24,1536]{6,5,4,3,2,1,0:T(8,128)(2,1)S(1)}, u32[]{:S(2)}, u32[]{:S(2)}) collective-permute-start(bf16[2,1,1,1,1,24,1536]{6,5,4,3,2,1,0:T(8,128)(2,1)S(1)} %pad_maximum_fusion.21), channel_id=1, source_target_pairs={{0,8},{2,10},{4,12},{6,14},{8,0},{10,2},{12,4},{14,6},{16,24},{18,... | collective-permute-start | bytes 442376 | tf_op jit(solution)/shard_map/ppermute | solution.py:70
  78.7 11.3 %collective-permute-start.21 = (bf16[2,2,1,1,1,24,1536]{6,5,4,3,2,1,0:T(8,128)(2,1)S(1)}, bf16[2,2,1,1,1,24,1536]{6,5,4,3,2,1,0:T(8,128)(2,1)S(1)}, u32[]{:S(2)}, u32[]{:S(2)}) collective-permute-start(bf16[2,2,1,1,1,24,1536]{6,5,4,3,2,1,0:T(8,128)(2,1)S(1)} %pad_maximum_fusion.17), channel_id=1, source_target_pairs={{0,4},{2,6},{4,0},{6,2},{8,12},{10,14},{12,8},{14,10},{16,20},{18,... | collective-permute-start | bytes 884744 | tf_op jit(solution)/shard_map/ppermute | solution.py:70
  89.3 12.8 %collective-permute-start.24 = (bf16[512,1536]{1,0:T(8,128)(2,1)S(1)}, bf16[512,1536]{1,0:T(8,128)(2,1)S(1)}, u32[]{:S(2)}, u32[]{:S(2)}) collective-permute-start(bf16[512,1536]{1,0:T(8,128)(2,1)S(1)} %get-tuple-element.196.refs_1_.refs_2_.refs_4_.refs_5_), channel_id=1, source_target_pairs={{0,2},{2,0},{4,6},{6,4},{8,10},{10,8},{12,14},{14,12},{16,18},{18,... | collective-permute-start | bytes 4718600 | tf_op jit(solution)/shard_map/ppermute | solution.py:70
  89.7 11.4 %collective-permute-start.23 = (bf16[2,2,1,1,64,768]{5,4,3,2,1,0:T(8,128)(2,1)S(1)}, bf16[2,2,1,1,64,768]{5,4,3,2,1,0:T(8,128)(2,1)S(1)}, u32[]{:S(2)}, u32[]{:S(2)}) collective-permute-start(bf16[2,2,1,1,64,768]{5,4,3,2,1,0:T(8,128)(2,1)S(1)} %pad_maximum_fusion.14), channel_id=1, source_target_pairs={{0,1},{1,0},{2,3},{3,2},{4,5},{5,4},{6,7},{7,6},{8,9},{9,8},{10,11... | collective-permute-start | bytes 1179656 | tf_op jit(solution)/shard_map/ppermute | solution.py:70
  102.1 28.6 %collective-permute-start.25 = (bf16[2,2,2,1,1,24,1536]{6,5,4,3,2,1,0:T(8,128)(2,1)}, bf16[2,2,2,1,1,24,1536]{6,5,4,3,2,1,0:T(8,128)(2,1)}, u32[]{:S(2)}, u32[]{:S(2)}) collective-permute-start(bf16[2,2,2,1,1,24,1536]{6,5,4,3,2,1,0:T(8,128)(2,1)} %pad_maximum_fusion.13), channel_id=1, source_target_pairs={{0,1},{1,0},{2,3},{3,2},{4,5},{5,4},{6,7},{7,6},{8,9},{9,8},{10,11... | collective-permute-start | bytes 1769480 | tf_op jit(solution)/shard_map/ppermute | solution.py:70
  104.6 30.4 %collective-permute-start.26 = (bf16[2,2,1,1,64,1536]{5,4,3,2,1,0:T(8,128)(2,1)}, bf16[2,2,1,1,64,1536]{5,4,3,2,1,0:T(8,128)(2,1)S(1)}, u32[]{:S(2)}, u32[]{:S(2)}) collective-permute-start(bf16[2,2,1,1,64,1536]{5,4,3,2,1,0:T(8,128)(2,1)} %pad_maximum_fusion.8), channel_id=1, source_target_pairs={{0,4},{2,6},{4,0},{6,2},{8,12},{10,14},{12,8},{14,10},{16,20},{18,... | collective-permute-start | bytes 2359304 | tf_op jit(solution)/shard_map/ppermute | solution.py:70
  135.4 5.9 %collective-permute-start.28 = (bf16[2,2,2,1,2,24,1536]{6,5,4,3,2,1,0:T(8,128)(2,1)S(1)}, bf16[2,2,2,1,2,24,1536]{6,5,4,3,2,1,0:T(8,128)(2,1)S(1)}, u32[]{:S(2)}, u32[]{:S(2)}) collective-permute-start(bf16[2,2,2,1,2,24,1536]{6,5,4,3,2,1,0:T(8,128)(2,1)S(1)} %pad_maximum_fusion.7), channel_id=1, source_target_pairs={{0,2},{2,0},{4,6},{6,4},{8,10},{10,8},{12,14},{14,12},{16,18},{18,... | collective-permute-start | bytes 3538952 | tf_op jit(solution)/shard_map/ppermute | solution.py:70
  138.2 8.7 %collective-permute-start.30 = (bf16[2,2,2,1,64,1536]{5,4,3,2,1,0:T(8,128)(2,1)S(1)}, bf16[2,2,2,1,64,1536]{5,4,3,2,1,0:T(8,128)(2,1)S(1)}, u32[]{:S(2)}, u32[]{:S(2)}) collective-permute-start(bf16[2,2,2,1,64,1536]{5,4,3,2,1,0:T(8,128)(2,1)S(1)} %pad_maximum_fusion.4), channel_id=1, source_target_pairs={{0,2},{2,0},{4,6},{6,4},{8,10},{10,8},{12,14},{14,12},{16,18},{18,... | collective-permute-start | bytes 4718600 | tf_op jit(solution)/shard_map/ppermute | solution.py:70
  140.5 14.1 %collective-permute-start.31 = (bf16[512,768]{1,0:T(8,128)(2,1)S(1)}, bf16[512,768]{1,0:T(8,128)(2,1)S(1)}, u32[]{:S(2)}, u32[]{:S(2)}) collective-permute-start(bf16[512,768]{1,0:T(8,128)(2,1)S(1)} %bitcast.98), channel_id=1, source_target_pairs={{1,2},{2,1},{5,6},{6,5},{9,10},{10,9},{13,14},{14,13},{17,18},{18,... | collective-permute-start | bytes 2359304 | tf_op jit(solution)/shard_map/ppermute | solution.py:159
  183.7 143.6 %reduce-scatter.5.cloned.1.call-start = ((), (), s32[]{:S(2)}) async-start(), calls=%async_computation.4 | async-start | bytes 1474560 | tf_op jit(solution)/shard_map/reduce_scatter | solution.py:1162
  235.8 8.9 %collective-permute-start.34 = (bf16[2,2,2,1,2,24,1536]{6,5,4,3,2,1,0:T(8,128)(2,1)}, bf16[2,2,2,1,2,24,1536]{6,5,4,3,2,1,0:T(8,128)(2,1)}, u32[]{:S(2)}, u32[]{:S(2)}) collective-permute-start(bf16[2,2,2,1,2,24,1536]{6,5,4,3,2,1,0:T(8,128)(2,1)} %constant_dynamic-slice_fusion.18), channel_id=1, source_target_pairs={{0,2},{2,0},{4,6},{6,4},{8,10},{10,8},{12,14},{14,12},{16,18},{18,... | collective-permute-start | bytes 3538952 | tf_op jit(solution)/shard_map/ppermute | solution.py:70
  237.3 9.4 %collective-permute-start.33 = (bf16[2,2,2,1,2,24,1536]{6,5,4,3,2,1,0:T(8,128)(2,1)}, bf16[2,2,2,1,2,24,1536]{6,5,4,3,2,1,0:T(8,128)(2,1)}, u32[]{:S(2)}, u32[]{:S(2)}) collective-permute-start(bf16[2,2,2,1,2,24,1536]{6,5,4,3,2,1,0:T(8,128)(2,1)} %constant_dynamic-slice_fusion.19), channel_id=1, source_target_pairs={{0,2},{2,0},{4,6},{6,4},{8,10},{10,8},{12,14},{14,12},{16,18},{18,... | collective-permute-start | bytes 3538952 | tf_op jit(solution)/shard_map/ppermute | solution.py:70
  249.7 28.8 %collective-permute-start.39 = (bf16[2,2,2,1,64,1536]{5,4,3,2,1,0:T(8,128)(2,1)}, bf16[2,2,2,1,64,1536]{5,4,3,2,1,0:T(8,128)(2,1)S(1)}, u32[]{:S(2)}, u32[]{:S(2)}) collective-permute-start(bf16[2,2,2,1,64,1536]{5,4,3,2,1,0:T(8,128)(2,1)} %constant_dynamic-slice_fusion.14), channel_id=1, source_target_pairs={{0,2},{2,0},{4,6},{6,4},{8,10},{10,8},{12,14},{14,12},{16,18},{18,... | collective-permute-start | bytes 4718600 | tf_op jit(solution)/shard_map/ppermute | solution.py:70
  251.2 24.6 %collective-permute-start.38 = (bf16[2,2,2,1,2,24,1536]{6,5,4,3,2,1,0:T(8,128)(2,1)}, bf16[2,2,2,1,2,24,1536]{6,5,4,3,2,1,0:T(8,128)(2,1)}, u32[]{:S(2)}, u32[]{:S(2)}) collective-permute-start(bf16[2,2,2,1,2,24,1536]{6,5,4,3,2,1,0:T(8,128)(2,1)} %constant_dynamic-slice_fusion.15), channel_id=1, source_target_pairs={{0,2},{2,0},{4,6},{6,4},{8,10},{10,8},{12,14},{14,12},{16,18},{18,... | collective-permute-start | bytes 3538952 | tf_op jit(solution)/shard_map/ppermute | solution.py:70
  251.4 21.4 %collective-permute-start.37 = (bf16[2,2,1,1,2,24,1536]{6,5,4,3,2,1,0:T(8,128)(2,1)S(1)}, bf16[2,2,1,1,2,24,1536]{6,5,4,3,2,1,0:T(8,128)(2,1)}, u32[]{:S(2)}, u32[]{:S(2)}) collective-permute-start(bf16[2,2,1,1,2,24,1536]{6,5,4,3,2,1,0:T(8,128)(2,1)S(1)} %constant_dynamic-slice_fusion.16), channel_id=1, source_target_pairs={{0,4},{2,6},{4,0},{6,2},{8,12},{10,14},{12,8},{14,10},{16,20},{18,... | collective-permute-start | bytes 1769480 | tf_op jit(solution)/shard_map/ppermute | solution.py:70
  257.0 17.9 %collective-permute-start.36 = (bf16[2,2,2,1,1,24,1536]{6,5,4,3,2,1,0:T(8,128)(2,1)S(1)}, bf16[2,2,2,1,1,24,1536]{6,5,4,3,2,1,0:T(8,128)(2,1)S(1)}, u32[]{:S(2)}, u32[]{:S(2)}) collective-permute-start(bf16[2,2,2,1,1,24,1536]{6,5,4,3,2,1,0:T(8,128)(2,1)S(1)} %constant_dynamic-slice_fusion.17), channel_id=1, source_target_pairs={{0,1},{1,0},{2,3},{3,2},{4,5},{5,4},{6,7},{7,6},{8,9},{9,8},{10,11... | collective-permute-start | bytes 1769480 | tf_op jit(solution)/shard_map/ppermute | solution.py:70
  279.9 28.3 %collective-permute-start.45 = (bf16[2,2,1,1,64,1536]{5,4,3,2,1,0:T(8,128)(2,1)}, bf16[2,2,1,1,64,1536]{5,4,3,2,1,0:T(8,128)(2,1)}, u32[]{:S(2)}, u32[]{:S(2)}) collective-permute-start(bf16[2,2,1,1,64,1536]{5,4,3,2,1,0:T(8,128)(2,1)} %constant_dynamic-slice_fusion.10), channel_id=1, source_target_pairs={{0,4},{2,6},{4,0},{6,2},{8,12},{10,14},{12,8},{14,10},{16,20},{18,... | collective-permute-start | bytes 2359304 | tf_op jit(solution)/shard_map/ppermute | solution.py:70
  281.3 25.7 %collective-permute-start.44 = (bf16[2,2,2,1,1,24,1536]{6,5,4,3,2,1,0:T(8,128)(2,1)}, bf16[2,2,2,1,1,24,1536]{6,5,4,3,2,1,0:T(8,128)(2,1)}, u32[]{:S(2)}, u32[]{:S(2)}) collective-permute-start(bf16[2,2,2,1,1,24,1536]{6,5,4,3,2,1,0:T(8,128)(2,1)} %constant_dynamic-slice_fusion.11), channel_id=1, source_target_pairs={{0,1},{1,0},{2,3},{3,2},{4,5},{5,4},{6,7},{7,6},{8,9},{9,8},{10,11... | collective-permute-start | bytes 1769480 | tf_op jit(solution)/shard_map/ppermute | solution.py:70
  286.2 16.9 %collective-permute-start.43 = (bf16[2,2,1,1,1,24,1536]{6,5,4,3,2,1,0:T(8,128)(2,1)S(1)}, bf16[2,2,1,1,1,24,1536]{6,5,4,3,2,1,0:T(8,128)(2,1)}, u32[]{:S(2)}, u32[]{:S(2)}) collective-permute-start(bf16[2,2,1,1,1,24,1536]{6,5,4,3,2,1,0:T(8,128)(2,1)S(1)} %constant_dynamic-slice_fusion.12), channel_id=1, source_target_pairs={{0,1},{1,0},{2,3},{3,2},{4,5},{5,4},{6,7},{7,6},{8,9},{9,8},{10,11... | collective-permute-start | bytes 884744 | tf_op jit(solution)/shard_map/ppermute | solution.py:70
  289.8 16.1 %collective-permute-start.42 = (bf16[2,2,1,1,1,24,1536]{6,5,4,3,2,1,0:T(8,128)(2,1)}, bf16[2,2,1,1,1,24,1536]{6,5,4,3,2,1,0:T(8,128)(2,1)}, u32[]{:S(2)}, u32[]{:S(2)}) collective-permute-start(bf16[2,2,1,1,1,24,1536]{6,5,4,3,2,1,0:T(8,128)(2,1)} %constant_dynamic-slice_fusion.13), channel_id=1, source_target_pairs={{0,4},{2,6},{4,0},{6,2},{8,12},{10,14},{12,8},{14,10},{16,20},{18,... | collective-permute-start | bytes 884744 | tf_op jit(solution)/shard_map/ppermute | solution.py:70
  309.6 17.5 %collective-permute-start.51 = (bf16[2,2,1,1,64,768]{5,4,3,2,1,0:T(8,128)(2,1)S(1)}, bf16[2,2,1,1,64,768]{5,4,3,2,1,0:T(8,128)(2,1)S(1)}, u32[]{:S(2)}, u32[]{:S(2)}) collective-permute-start(bf16[2,2,1,1,64,768]{5,4,3,2,1,0:T(8,128)(2,1)S(1)} %constant_dynamic-slice_fusion.6), channel_id=1, source_target_pairs={{0,1},{1,0},{2,3},{3,2},{4,5},{5,4},{6,7},{7,6},{8,9},{9,8},{10,11... | collective-permute-start | bytes 1179656 | tf_op jit(solution)/shard_map/ppermute | solution.py:70
  311.1 15.9 %collective-permute-start.50 = (bf16[2,2,1,1,1,24,1536]{6,5,4,3,2,1,0:T(8,128)(2,1)S(1)}, bf16[2,2,1,1,1,24,1536]{6,5,4,3,2,1,0:T(8,128)(2,1)S(1)}, u32[]{:S(2)}, u32[]{:S(2)}) collective-permute-start(bf16[2,2,1,1,1,24,1536]{6,5,4,3,2,1,0:T(8,128)(2,1)S(1)} %constant_dynamic-slice_fusion.7), channel_id=1, source_target_pairs={{0,4},{2,6},{4,0},{6,2},{8,12},{10,14},{12,8},{14,10},{16,20},{18,... | collective-permute-start | bytes 884744 | tf_op jit(solution)/shard_map/ppermute | solution.py:70
  311.9 9.5 %collective-permute-start.49 = (bf16[2,1,1,1,1,24,1536]{6,5,4,3,2,1,0:T(8,128)(2,1)S(1)}, bf16[2,1,1,1,1,24,1536]{6,5,4,3,2,1,0:T(8,128)(2,1)S(1)}, u32[]{:S(2)}, u32[]{:S(2)}) collective-permute-start(bf16[2,1,1,1,1,24,1536]{6,5,4,3,2,1,0:T(8,128)(2,1)S(1)} %constant_dynamic-slice_fusion.8), channel_id=1, source_target_pairs={{0,8},{2,10},{4,12},{6,14},{8,0},{10,2},{12,4},{14,6},{16,24},{18,... | collective-permute-start | bytes 442376 | tf_op jit(solution)/shard_map/ppermute | solution.py:70
  313.4 7.0 %collective-permute-start.46 = (f32[2,2,1,1,4608]{4,3,2,1,0:T(1,128)S(1)}, f32[2,2,1,1,4608]{4,3,2,1,0:T(1,128)S(1)}, u32[]{:S(2)}, u32[]{:S(2)}) collective-permute-start(f32[2,2,1,1,4608]{4,3,2,1,0:T(1,128)S(1)} %pad_maximum_fusion.24), channel_id=1, source_target_pairs={{0,4},{2,6},{4,0},{6,2},{8,12},{10,14},{12,8},{14,10},{16,20},{18,... | collective-permute-start | bytes 221192 | tf_op jit(solution)/shard_map/ppermute | solution.py:70
  314.8 8.2 %collective-permute-start.48 = (bf16[2,1,1,1,1,24,1536]{6,5,4,3,2,1,0:T(8,128)(2,1)S(1)}, bf16[2,1,1,1,1,24,1536]{6,5,4,3,2,1,0:T(8,128)(2,1)S(1)}, u32[]{:S(2)}, u32[]{:S(2)}) collective-permute-start(bf16[2,1,1,1,1,24,1536]{6,5,4,3,2,1,0:T(8,128)(2,1)S(1)} %constant_dynamic-slice_fusion.9), channel_id=1, source_target_pairs={{0,8},{2,10},{4,12},{6,14},{8,0},{10,2},{12,4},{14,6},{16,24},{18,... | collective-permute-start | bytes 442376 | tf_op jit(solution)/shard_map/ppermute | solution.py:70
  329.0 12.6 %collective-permute-start.55 = (bf16[2,1,1,1,64,768]{5,4,3,2,1,0:T(8,128)(2,1)}, bf16[2,1,1,1,64,768]{5,4,3,2,1,0:T(8,128)(2,1)}, u32[]{:S(2)}, u32[]{:S(2)}) collective-permute-start(bf16[2,1,1,1,64,768]{5,4,3,2,1,0:T(8,128)(2,1)} %constant_dynamic-slice_fusion.2), channel_id=1, source_target_pairs={{0,8},{2,10},{4,12},{6,14},{8,0},{10,2},{12,4},{14,6},{16,24},{18,... | collective-permute-start | bytes 589832 | tf_op jit(solution)/shard_map/ppermute | solution.py:70
  330.6 10.1 %collective-permute-start.54 = (bf16[2,1,1,1,1,24,1536]{6,5,4,3,2,1,0:T(8,128)(2,1)S(1)}, bf16[2,1,1,1,1,24,1536]{6,5,4,3,2,1,0:T(8,128)(2,1)}, u32[]{:S(2)}, u32[]{:S(2)}) collective-permute-start(bf16[2,1,1,1,1,24,1536]{6,5,4,3,2,1,0:T(8,128)(2,1)S(1)} %constant_dynamic-slice_fusion.3), channel_id=1, source_target_pairs={{0,8},{2,10},{4,12},{6,14},{8,0},{10,2},{12,4},{14,6},{16,24},{18,... | collective-permute-start | bytes 442376 | tf_op jit(solution)/shard_map/ppermute | solution.py:70
  331.8 6.3 %collective-permute-start.53 = (bf16[1,1,1,1,1,24,1536]{6,5,4,3,2,1,0:T(8,128)(2,1)}, bf16[1,1,1,1,1,24,1536]{6,5,4,3,2,1,0:T(8,128)(2,1)}, u32[]{:S(2)}, u32[]{:S(2)}) collective-permute-start(bf16[1,1,1,1,1,24,1536]{6,5,4,3,2,1,0:T(8,128)(2,1)} %constant_dynamic-slice_fusion.4), channel_id=1, source_target_pairs={{0,16},{2,18},{4,20},{6,22},{8,24},{10,26},{12,28},{14,30},{16,0},... | collective-permute-start | bytes 221192 | tf_op jit(solution)/shard_map/ppermute | solution.py:70
  342.6 6.1 %collective-permute-start.56 = (bf16[1,1,1,1,1,24,1536]{6,5,4,3,2,1,0:T(8,128)(2,1)S(1)}, bf16[1,1,1,1,1,24,1536]{6,5,4,3,2,1,0:T(8,128)(2,1)S(1)}, u32[]{:S(2)}, u32[]{:S(2)}) collective-permute-start(bf16[1,1,1,1,1,24,1536]{6,5,4,3,2,1,0:T(8,128)(2,1)S(1)} %constant_dynamic-slice_fusion.1), channel_id=1, source_target_pairs={{0,16},{2,18},{4,20},{6,22},{8,24},{10,26},{12,28},{14,30},{16,0},... | collective-permute-start | bytes 221192 | tf_op jit(solution)/shard_map/ppermute | solution.py:70
  344.8 7.0 %collective-permute-start.57 = (bf16[1,1,1,1,64,768]{5,4,3,2,1,0:T(8,128)(2,1)S(1)}, bf16[1,1,1,1,64,768]{5,4,3,2,1,0:T(8,128)(2,1)S(1)}, u32[]{:S(2)}, u32[]{:S(2)}) collective-permute-start(bf16[1,1,1,1,64,768]{5,4,3,2,1,0:T(8,128)(2,1)S(1)} %constant_dynamic-slice_fusion), channel_id=1, source_target_pairs={{0,16},{2,18},{4,20},{6,22},{8,24},{10,26},{12,28},{14,30},{16,0},... | collective-permute-start | bytes 294920 | tf_op jit(solution)/shard_map/ppermute | solution.py:70
  345.7 49.0 %collective-permute-start.69 = (bf16[512,768]{1,0:T(8,128)(2,1)S(1)}, bf16[512,768]{1,0:T(8,128)(2,1)}, u32[]{:S(2)}, u32[]{:S(2)}) collective-permute-start(bf16[512,768]{1,0:T(8,128)(2,1)S(1)} %copy-done.34), channel_id=1, source_target_pairs={{1,2},{2,1},{5,6},{6,5},{9,10},{10,9},{13,14},{14,13},{17,18},{18,... | collective-permute-start | bytes 2359304 | tf_op jit(solution)/shard_map/ppermute | solution.py:159
  347.2 48.4 %collective-permute-start.68 = (bf16[512,768]{1,0:T(8,128)(2,1)S(1)}, bf16[512,768]{1,0:T(8,128)(2,1)}, u32[]{:S(2)}, u32[]{:S(2)}) collective-permute-start(bf16[512,768]{1,0:T(8,128)(2,1)S(1)} %copy-done.32), channel_id=1, source_target_pairs={{1,2},{2,1},{5,6},{6,5},{9,10},{10,9},{13,14},{14,13},{17,18},{18,... | collective-permute-start | bytes 2359304 | tf_op jit(solution)/shard_map/ppermute | solution.py:159
  363.6 6.5 %collective-permute-start.61 = (f32[184,128]{1,0:T(8,128)S(1)}, f32[184,128]{1,0:T(8,128)S(1)}, u32[]{:S(2)}, u32[]{:S(2)}) collective-permute-start(f32[184,128]{1,0:T(8,128)S(1)} %add.462), channel_id=1, source_target_pairs={{0,16},{2,18},{4,20},{6,22},{8,24},{10,26},{12,28},{14,30},{16,0},... | collective-permute-start | bytes 282632 | tf_op jit(solution)/shard_map/ppermute | solution.py:70
  (94 other events, 549.0 us)
Sparse Core Ops, SparseCore 0:
  44.0 100.9 all-gather.1
  183.8 83.3 reduce-scatter.2
  291.4 29.7 reduce-scatter.4
where the time goes:
time: 414 us; the launch traced here: 406 us
  waiting for transfers between devices  138 us (33%)
  Pallas kernels  98.3 us (24%)
  starting transfers between devices  69.7 us (17%)
  other arithmetic  44.4 us (11%)
  local copies, waits for them, and re-layouts  37.2 us (9%)
  between operations  16.3 us (4%)
    ppermute x64, waiting for transfers between devices, cross(): return lax.ppermute(values, link[0], pairs)  135 us
    ppermute x64, starting transfers between devices, cross(): return lax.ppermute(values, link[0], pairs)  60.4 us
    pallas_call x2, Pallas kernels, attend_back(): pl.pallas_call(functools.partial(back_kernel, blocks, places), grid=(PAIR...  27.9 us
    pallas_call x1, Pallas kernels, mlp_both(): pl.pallas_call(mlp_kernel, grid=(2, tiles), in_specs=[whole, pl.BlockSpec...  25 us
    unnamed x145, local copies, waits for them, and re-layouts  21.1 us
    pallas_call x4, Pallas kernels, frame_call(): pl.pallas_call(kernel, grid=(1,), in_specs=specs, out_specs=[whole_block(...  19.6 us
    convert_element_type x16, other arithmetic, shrink(): (kept.astype(FLOAT) + cross(sent.astype(BFLOAT), link).astype(FLOAT)).ast...  16.7 us
    pallas_call x2, Pallas kernels, attend(): pl.pallas_call(functools.partial(attend_kernel, blocks), grid=(PAIRS // c...  16.1 us
  transfers between devices with their start and end apart: 73, of which 36 were waited for; matrix products, arithmetic and copies ran while one was open for 14% of the time, Pallas kernels for 18%

commit v1 on v0

--- a/solution.py
+++ b/solution.py
@@ -656,12 +656,16 @@
     in_ref,
     modulation_ref,
     query_weight_ref,
+    text_ref,
+    text_weight_ref,
     branch_ref,
     after_ref,
     cross_input_ref,
     query_ref,
+    text_pair_ref,
 ):
     branch_ref[...] = nn(attn_ref[...], project_ref[...])
+    text_pair_ref[...] = nn(text_ref[...], text_weight_ref[...]).astype(BFLOAT)
     gate = block_of(modulation_ref, GATE_SELF)
 
     def some(rows, carry):
@@ -1053,17 +1057,24 @@
     swapped_cotangent = swap_only(cotangent[0])
     cross_pair, w_text = [chain.finish() for chain in second]
     cross_pair, w_text = cross_pair.reshape(D, 2 * D), w_text.reshape(DT, 2 * D)
-    self_branch, after_self, cross_input, cross_query = frame_call(
+    self_branch, after_self, cross_input, cross_query, text_pair = frame_call(
         between_kernel,
-        [(square, FLOAT), (square, FLOAT), (square, BFLOAT), (square, BFLOAT)],
+        [
+            (square, FLOAT),
+            (square, FLOAT),
+            (square, BFLOAT),
+            (square, BFLOAT),
+            ((clip_text.shape[0], 2 * D), BFLOAT),
+        ],
         self_attn,
         right_half(query_out),
         inputs,
         modulation,
         left_half(cross_pair),
-    )
-
-    text_pair = nn(clip_text, w_text).astype(BFLOAT)
+        clip_text,
+        w_text,
+    )
+
     text_keys = [(text_pair, text_bias)]
     cross_attn, cross_logs = attend(cross_query, text_keys, half_places, PAIRS // 2)
 

time: 414 us -> 415 us (level)
    unnamed x145 -> x159, local copies, waits for them, and re-layouts: 21.1 us -> 22.2 us
where the time goes in v1:
time: 415 us; the launch traced here: 407 us
  waiting for transfers between devices  134 us (32%)
  Pallas kernels  101 us (24%)
  starting transfers between devices  72.3 us (17%)
  other arithmetic  44.3 us (11%)
  local copies, waits for them, and re-layouts  38.1 us (9%)
  between operations  16.4 us (4%)
    ppermute x64, waiting for transfers between devices, cross(): return lax.ppermute(values, link[0], pairs)  131 us
    ppermute x64, starting transfers between devices, cross(): return lax.ppermute(values, link[0], pairs)  63.3 us
    pallas_call x2, Pallas kernels, attend_back(): pl.pallas_call(functools.partial(back_kernel, blocks, places), grid=(PAIR...  28 us
    pallas_call x1, Pallas kernels, mlp_both(): pl.pallas_call(mlp_kernel, grid=(2, tiles), in_specs=[whole, pl.BlockSpec...  25.1 us
    unnamed x159, local copies, waits for them, and re-layouts  22.2 us
    pallas_call x4, Pallas kernels, frame_call(): pl.pallas_call(kernel, grid=(1,), in_specs=specs, out_specs=[whole_block(...  21.7 us
    pallas_call x2, Pallas kernels, attend(): pl.pallas_call(functools.partial(attend_kernel, blocks), grid=(PAIRS // c...  16.1 us
    convert_element_type x16, other arithmetic, shrink(): (kept.astype(FLOAT) + cross(sent.astype(BFLOAT), link).astype(FLOAT)).ast...  14.1 us
  transfers between devices with their start and end apart: 73, of which 36 were waited for; matrix products, arithmetic and copies ran while one was open for 14% of the time, Pallas kernels for 18%

profile of v1, /device:TPU:0, one launch (start us, length us, event | category | flops | bytes accessed | tf_op | source)
XLA Modules:
  0.0 407.2 jit_solution(14652523806182641855)
XLA Ops:
  9.2 4.1 %collective-permute-start.2 = (bf16[1,1,1,1,1,24,3072]{6,5,4,3,2,1,0:T(8,128)(2,1)S(1)}, bf16[1,1,1,1,1,24,3072]{6,5,4,3,2,1,0:T(8,128)(2,1)S(1)}, u32[]{:S(2)}, u32[]{:S(2)}) collective-permute-start(bf16[1,1,1,1,1,24,3072]{6,5,4,3,2,1,0:T(8,128)(2,1)S(1)} %pad_maximum_fusion.20), channel_id=1, source_target_pairs={{0,16},{2,18},{4,20},{6,22},{8,24},{10,26},{12,28},{14,30},{16,0},... | collective-permute-start | bytes 442376 | tf_op jit(solution)/shard_map/ppermute | solution.py:70
  19.8 2.0 collective-permute-done.1
  25.4 5.5 %collective-permute-done.3 = s32[16]{0:T(128)S(1)} collective-permute-done((s32[16]{0:T(128)S(1)}, s32[16]{0:T(128)S(1)}, u32[]{:S(2)}, u32[]{:S(2)}) %collective-permute-start.3) | collective-permute-done | bytes 96 | tf_op jit(solution)/shard_map/ppermute | solution.py:70
  32.3 2.0 collective-permute-done.4
  34.6 3.4 collective-permute-start.11
  43.4 2.3 collective-permute-done.10
  45.8 6.1 %collective-permute-done.7 = f32[8,1,4608]{2,1,0:T(1,128)S(1)} collective-permute-done((f32[8,1,4608]{2,1,0:T(1,128)S(1)}, f32[8,1,4608]{2,1,0:T(1,128)S(1)}, u32[]{:S(2)}, u32[]{:S(2)}) %collective-permute-start.7) | collective-permute-done | bytes 147488 | tf_op jit(solution)/shard_map/ppermute | solution.py:70
  53.9 4.4 %collective-permute-done.12 = f32[2,1,2,4608]{3,2,1,0:T(2,128)S(1)} collective-permute-done((f32[2,1,2,4608]{3,2,1,0:T(2,128)S(1)}, f32[2,1,2,4608]{3,2,1,0:T(2,128)S(1)}, u32[]{:S(2)}, u32[]{:S(2)}) %collective-permute-start.12) | collective-permute-done | bytes 73760 | tf_op jit(solution)/shard_map/ppermute | solution.py:70
  58.4 3.5 collective-permute-start.13
  65.2 12.5 %collective-permute-done.15 = bf16[2,2,1,1,2,24,1536]{6,5,4,3,2,1,0:T(8,128)(2,1)S(1)} collective-permute-done((bf16[2,2,1,1,2,24,1536]{6,5,4,3,2,1,0:T(8,128)(2,1)S(1)}, bf16[2,2,1,1,2,24,1536]{6,5,4,3,2,1,0:T(8,128)(2,1)S(1)}, u32[]{:S(2)}, u32[]{:S(2)}) %collective-permute-start.15) | collective-permute-done | bytes 589856 | tf_op jit(solution)/shard_map/ppermute | solution.py:70
  78.1 2.0 collective-permute-start.16
  80.2 2.1 collective-permute-done.16
  88.8 4.4 %shard_map.320 = (bf16[512,768]{1,0:T(8,128)(2,1)S(1)}, bf16[512,768]{1,0:T(8,128)(2,1)S(1)}, bf16[512,1536]{1,0:T(8,128)(2,1)S(1)}) custom-call(bf16[512,768]{1,0:T(8,128)(2,1)S(1)} %broadcast_select_fusion.12.in_ref, f32[1,4608]{1,0:T(1,128)S(1)} %add_bitcast_fusion.1.modulation_ref, bf16[768,1536]{1,0:T(8,128)(2,1)} %bitcast.80, bf16[768,1536]{1,0:T(8,128)(2,1)} %bitcast.89), custom_call_target="tpu_custom_call" | custom-call | flops 1000 | bytes 1000 | tf_op jit(solution)/shard_map/pallas_call | solution.py:845
  95.1 17.1 %collective-permute-done.23 = bf16[2,2,1,1,64,768]{5,4,3,2,1,0:T(8,128)(2,1)S(1)} collective-permute-done((bf16[2,2,1,1,64,768]{5,4,3,2,1,0:T(8,128)(2,1)S(1)}, bf16[2,2,1,1,64,768]{5,4,3,2,1,0:T(8,128)(2,1)S(1)}, u32[]{:S(2)}, u32[]{:S(2)}) %collective-permute-start.23) | collective-permute-done | bytes 393248 | tf_op jit(solution)/shard_map/ppermute | solution.py:70
  116.8 11.3 %shard_map.321 = (bf16[512,768]{1,0:T(8,128)(2,1)S(1)}, f32[6,2,512]{2,1,0:T(2,128)S(1)}) custom-call(bf16[512,768]{1,0:T(8,128)(2,1)S(1)} %copy-done.16, bf16[512,1536]{1,0:T(8,128)(2,1)S(1)} %get-tuple-element.197.refs_1_.refs_2_.refs_4_.refs_5_, bf16[512,1536]{1,0:T(8,128)(2,1)S(1)} %get-tuple-element.197.refs_1_.refs_2_.refs_4_.refs_5_, ...), custom_call_target="tpu_custom_call" | custom-call | flops 1000 | bytes 1000 | tf_op jit(solution)/shard_map/pallas_call | solution.py:322
  128.1 6.4 %collective-permute-done.25 = bf16[2,2,2,1,1,24,1536]{6,5,4,3,2,1,0:T(8,128)(2,1)} collective-permute-done((bf16[2,2,2,1,1,24,1536]{6,5,4,3,2,1,0:T(8,128)(2,1)}, bf16[2,2,2,1,1,24,1536]{6,5,4,3,2,1,0:T(8,128)(2,1)}, u32[]{:S(2)}, u32[]{:S(2)}) %collective-permute-start.25) | collective-permute-done | bytes 589856 | tf_op jit(solution)/shard_map/ppermute | solution.py:70
  140.0 2.1 collective-permute-done.29
  145.2 2.0 pad_maximum_fusion
  147.3 5.1 %shard_map.322 = (f32[512,768]{1,0:T(8,128)S(1)}, f32[512,768]{1,0:T(8,128)}, bf16[512,768]{1,0:T(8,128)(2,1)S(1)}, bf16[512,768]{1,0:T(8,128)(2,1)S(1)}, bf16[256,1536]{1,0:T(8,128)(2,1)S(1)}) custom-call(bf16[512,768]{1,0:T(8,128)(2,1)S(1)} %get-tuple-element.204.attn_ref.refs_1_.refs_2_, bf16[768,1536]{1,0:T(8,128)(2,1)} %bitcast.81, ...), custom_call_target="tpu_custom_call" | custom-call | flops 1000 | bytes 1000 | tf_op jit(solution)/shard_map/pallas_call | solution.py:845
  154.5 4.8 %shard_map.323 = (bf16[512,768]{1,0:T(8,128)(2,1)S(1)}, f32[6,2,512]{2,1,0:T(2,128)S(1)}) custom-call(bf16[512,768]{1,0:T(8,128)(2,1)S(1)} %get-tuple-element.210.refs_0_, bf16[256,1536]{1,0:T(8,128)(2,1)S(1)} %get-tuple-element.211.refs_1_.refs_2_.refs_4_.refs_5_, bf16[256,1536]{1,0:T(8,128)(2,1)S(1)} %get-tuple-element.211.refs_1_.refs_2_.refs_4_.refs_5_, ...), custom_call_target="tpu_custom_call" | custom-call | flops 1000 | bytes 1000 | tf_op jit(solution)/shard_map/pallas_call | solution.py:322
  159.4 25.1 %shard_map.324 = (bf16[512,768]{1,0:T(8,128)(2,1)S(1)}, f32[512,768]{1,0:T(8,128)S(1)}, bf16[512,768]{1,0:T(8,128)(2,1)S(1)}, bf16[512,768]{1,0:T(8,128)(2,1)S(1...) custom-call(bf16[512,768]{1,0:T(8,128)(2,1)S(1)} %get-tuple-element.214.attn_ref.refs_1_.refs_2_, ...), custom_call_target="tpu_custom_call" | custom-call | flops 1000 | bytes 1000 | tf_op jit(solution)/shard_map/pallas_call | solution.py:868
  191.3 6.8 %shard_map.325 = (bf16[512,768]{1,0:T(8,128)(2,1)S(1)}, bf16[256,1536]{1,0:T(8,128)(2,1)S(1)}) custom-call(bf16[512,768]{1,0:T(8,128)(2,1)S(1)} %copy-done.23, bf16[512,768]{1,0:T(8,128)(2,1)S(1)} %get-tuple-element.214.attn_ref.refs_1_.refs_2_, bf16[512,768]{1,0:T(8,128)(2,1)S(1)} %copy-done.43, f32[6,2,512]{2,1,0:T(2,128)S(1)} %get-tuple-element.220.refs_3_, ...), custom_call_target="tpu_custom_call" | custom-call | flops 1000 | bytes 1000 | tf_op jit(solution)/shard_map/pallas_call | solution.py:339
  199.0 6.5 %shard_map.326 = (f32[512,768]{1,0:T(8,128)S(1)}, bf16[512,768]{1,0:T(8,128)(2,1)S(1)}, bf16[512,768]{1,0:T(8,128)(2,1)S(1)}, f32[1,768]{1,0:T(1,128)S(1)}) custom-call(bf16[512,768]{1,0:T(8,128)(2,1)S(1)} %get-tuple-element.231.query_grad_ref.refs_1_, bf16[768,1536]{1,0:T(8,128)(2,1)} %bitcast.88, f32[512,768]{1,0:T(8,128)S(1)} %copy-done.10, ...), custom_call_target="tpu_custom_call" | custom-call | flops 1000 | bytes 1000 | tf_op jit(solution)/shard_map/pallas_call | solution.py:845
  206.7 21.2 %shard_map.327 = (bf16[512,768]{1,0:T(8,128)(2,1)S(1)}, bf16[512,1536]{1,0:T(8,128)(2,1)S(1)}, bf16[512,1536]{1,0:T(8,128)(2,1)}) custom-call(bf16[512,768]{1,0:T(8,128)(2,1)S(1)} %copy-done.17, bf16[512,768]{1,0:T(8,128)(2,1)S(1)} %copy-done.9, bf16[512,768]{1,0:T(8,128)(2,1)S(1)} %get-tuple-element.224.refs_2_, ...), custom_call_target="tpu_custom_call" | custom-call | flops 1000 | bytes 1000 | tf_op jit(solution)/shard_map/pallas_call | solution.py:339
  230.0 1.9 collective-permute-start.32
  235.3 2.5 add_convert_fusion.1.refs_1_.pair_grad_ref
  248.1 2.5 add_convert_fusion.3
  256.7 5.6 %shard_map.332 = (bf16[512,768]{1,0:T(8,128)(2,1)}, f32[1,1536]{1,0:T(1,128)S(1)}) custom-call(bf16[512,768]{1,0:T(8,128)(2,1)S(1)} %copy-done.26, bf16[512,1536]{1,0:T(8,128)(2,1)S(1)} %add_convert_fusion.1.refs_1_.pair_grad_ref, bf16[768,1536]{1,0:T(8,128)(2,1)} %bitcast.83, bf16[768,1536]{1,0:T(8,128)(2,1)} %bitcast.90, bf16[512,768]{1,0:T(8,128)(2,1)S(1)} %copy-done.3, ...), custom_call_target="tpu_custom_call" | custom-call | flops 1000 | bytes 1000 | tf_op jit(solution)/shard_map/pallas_call | solution.py:845
  263.7 11.8 %collective-permute-done.37 = bf16[2,2,1,1,2,24,1536]{6,5,4,3,2,1,0:T(8,128)(2,1)S(1)} collective-permute-done((bf16[2,2,1,1,2,24,1536]{6,5,4,3,2,1,0:T(8,128)(2,1)S(1)}, bf16[2,2,1,1,2,24,1536]{6,5,4,3,2,1,0:T(8,128)(2,1)S(1)}, u32[]{:S(2)}, u32[]{:S(2)}) %collective-permute-start.37) | collective-permute-done | bytes 589856 | tf_op jit(solution)/shard_map/ppermute | solution.py:70
  275.6 2.7 collective-permute-done.36
  286.9 3.5 collective-permute-done.40
  292.2 2.2 collective-permute-done.41
  294.6 10.7 %collective-permute-done.43 = bf16[2,2,1,1,1,24,1536]{6,5,4,3,2,1,0:T(8,128)(2,1)} collective-permute-done((bf16[2,2,1,1,1,24,1536]{6,5,4,3,2,1,0:T(8,128)(2,1)}, bf16[2,2,1,1,1,24,1536]{6,5,4,3,2,1,0:T(8,128)(2,1)}, u32[]{:S(2)}, u32[]{:S(2)}) %collective-permute-start.43) | collective-permute-done | bytes 294944 | tf_op jit(solution)/shard_map/ppermute | solution.py:70
  317.2 4.6 %collective-permute-done.46 = f32[2,2,1,1,4608]{4,3,2,1,0:T(1,128)S(1)} collective-permute-done((f32[2,2,1,1,4608]{4,3,2,1,0:T(1,128)S(1)}, f32[2,2,1,1,4608]{4,3,2,1,0:T(1,128)S(1)}, u32[]{:S(2)}, u32[]{:S(2)}) %collective-permute-start.46) | collective-permute-done | bytes 73760 | tf_op jit(solution)/shard_map/ppermute | solution.py:70
  324.0 3.2 collective-permute-done.47
  333.8 2.3 collective-permute-start.52
  336.1 1.9 reshape.232
  343.2 1.9 collective-permute-start.56
  349.4 2.9 collective-permute-done.57
  356.1 3.3 collective-permute-done.59
  361.0 3.0 collective-permute-done.60
  364.8 4.8 %collective-permute-done.61 = f32[184,128]{1,0:T(8,128)S(1)} collective-permute-done((f32[184,128]{1,0:T(8,128)S(1)}, f32[184,128]{1,0:T(8,128)S(1)}, u32[]{:S(2)}, u32[]{:S(2)}) %collective-permute-start.61) | collective-permute-done | bytes 94240 | tf_op jit(solution)/shard_map/ppermute | solution.py:70
  371.2 3.1 collective-permute-done.62
  374.3 2.1 shard_map.334
  381.1 2.1 collective-permute-done.64
  384.8 2.0 collective-permute-done.65
  387.9 3.3 collective-permute-done.66
  394.7 2.1 broadcast_select_fusion.8
  (429 shorter events, 142.2 us)
Async XLA Ops:
  7.2 152.2 %all-gather.2.cloned.1.call-start = ((), (), s32[]{:S(2)}) async-start(), calls=%async_computation.2 | async-start | bytes 9732096 | tf_op jit(solution)/shard_map/all_gather | solution.py:1019
  9.2 12.5 %collective-permute-start.2 = (bf16[1,1,1,1,1,24,3072]{6,5,4,3,2,1,0:T(8,128)(2,1)S(1)}, bf16[1,1,1,1,1,24,3072]{6,5,4,3,2,1,0:T(8,128)(2,1)S(1)}, u32[]{:S(2)}, u32[]{:S(2)}) collective-permute-start(bf16[1,1,1,1,1,24,3072]{6,5,4,3,2,1,0:T(8,128)(2,1)S(1)} %pad_maximum_fusion.20), channel_id=1, source_target_pairs={{0,16},{2,18},{4,20},{6,22},{8,24},{10,26},{12,28},{14,30},{16,0},... | collective-permute-start | bytes 442376 | tf_op jit(solution)/shard_map/ppermute | solution.py:70
  14.1 20.4 %collective-permute-start.6 = (bf16[512,768]{1,0:T(8,128)(2,1)}, bf16[512,768]{1,0:T(8,128)(2,1)}, u32[]{:S(2)}, u32[]{:S(2)}) collective-permute-start(bf16[512,768]{1,0:T(8,128)(2,1)} %bitcast.95), channel_id=1, source_target_pairs={{1,2},{2,1},{5,6},{6,5},{9,10},{10,9},{13,14},{14,13},{17,18},{18,... | collective-permute-start | bytes 2359304 | tf_op jit(solution)/shard_map/ppermute | solution.py:159
  21.9 12.5 %collective-permute-start.5 = (bf16[2,1,1,1,1,24,3072]{6,5,4,3,2,1,0:T(8,128)(2,1)S(1)}, bf16[2,1,1,1,1,24,3072]{6,5,4,3,2,1,0:T(8,128)(2,1)S(1)}, u32[]{:S(2)}, u32[]{:S(2)}) collective-permute-start(bf16[2,1,1,1,1,24,3072]{6,5,4,3,2,1,0:T(8,128)(2,1)S(1)} %pad_maximum_fusion.15), channel_id=1, source_target_pairs={{0,8},{2,10},{4,12},{6,14},{8,0},{10,2},{12,4},{14,6},{16,24},{18,... | collective-permute-start | bytes 884744 | tf_op jit(solution)/shard_map/ppermute | solution.py:70
  24.2 6.6 %collective-permute-start.3 = (s32[16]{0:T(128)S(1)}, s32[16]{0:T(128)S(1)}, u32[]{:S(2)}, u32[]{:S(2)}) collective-permute-start(s32[16]{0:T(128)S(1)} %add.409), channel_id=1, source_target_pairs={{0,16},{2,18},{4,20},{6,22},{8,24},{10,26},{12,28},{14,30},{16,0},... | collective-permute-start | bytes 200 | tf_op jit(solution)/shard_map/ppermute | solution.py:70
  34.6 11.0 %collective-permute-start.11 = (bf16[1,1,1,1,64,768]{5,4,3,2,1,0:T(8,128)(2,1)S(1)}, bf16[1,1,1,1,64,768]{5,4,3,2,1,0:T(8,128)(2,1)S(1)}, u32[]{:S(2)}, u32[]{:S(2)}) collective-permute-start(bf16[1,1,1,1,64,768]{5,4,3,2,1,0:T(8,128)(2,1)S(1)} %reshape_reshape.3), channel_id=1, source_target_pairs={{0,16},{2,18},{4,20},{6,22},{8,24},{10,26},{12,28},{14,30},{16,0},... | collective-permute-start | bytes 294920 | tf_op jit(solution)/shard_map/ppermute | solution.py:70
  38.0 7.6 %collective-permute-start.10 = (bf16[1,1,1,1,1,24,1536]{6,5,4,3,2,1,0:T(8,128)(2,1)S(1)}, bf16[1,1,1,1,1,24,1536]{6,5,4,3,2,1,0:T(8,128)(2,1)S(1)}, u32[]{:S(2)}, u32[]{:S(2)}) collective-permute-start(bf16[1,1,1,1,1,24,1536]{6,5,4,3,2,1,0:T(8,128)(2,1)S(1)} %pad_maximum_fusion.23), channel_id=1, source_target_pairs={{0,16},{2,18},{4,20},{6,22},{8,24},{10,26},{12,28},{14,30},{16,0},... | collective-permute-start | bytes 221192 | tf_op jit(solution)/shard_map/ppermute | solution.py:70
  39.0 13.5 %collective-permute-start.8 = (bf16[2,2,1,1,1,24,1536]{6,5,4,3,2,1,0:T(8,128)(2,1)}, bf16[2,2,1,1,1,24,1536]{6,5,4,3,2,1,0:T(8,128)(2,1)S(1)}, u32[]{:S(2)}, u32[]{:S(2)}) collective-permute-start(bf16[2,2,1,1,1,24,1536]{6,5,4,3,2,1,0:T(8,128)(2,1)} %get-tuple-element.342), channel_id=1, source_target_pairs={{0,4},{2,6},{4,0},{6,2},{8,12},{10,14},{12,8},{14,10},{16,20},{18,... | collective-permute-start | bytes 884744 | tf_op jit(solution)/shard_map/ppermute | solution.py:70
  40.5 12.0 %collective-permute-start.9 = (bf16[2,2,1,1,1,24,1536]{6,5,4,3,2,1,0:T(8,128)(2,1)}, bf16[2,2,1,1,1,24,1536]{6,5,4,3,2,1,0:T(8,128)(2,1)}, u32[]{:S(2)}, u32[]{:S(2)}) collective-permute-start(bf16[2,2,1,1,1,24,1536]{6,5,4,3,2,1,0:T(8,128)(2,1)} %get-tuple-element.341), channel_id=1, source_target_pairs={{0,1},{1,0},{2,3},{3,2},{4,5},{5,4},{6,7},{7,6},{8,9},{9,8},{10,11... | collective-permute-start | bytes 884744 | tf_op jit(solution)/shard_map/ppermute | solution.py:70
  42.8 9.1 %collective-permute-start.7 = (f32[8,1,4608]{2,1,0:T(1,128)S(1)}, f32[8,1,4608]{2,1,0:T(1,128)S(1)}, u32[]{:S(2)}, u32[]{:S(2)}) collective-permute-start(f32[8,1,4608]{2,1,0:T(1,128)S(1)} %constant_dynamic-slice_fusion.23), channel_id=1, source_target_pairs={{0,1},{1,0},{2,3},{3,2},{4,5},{5,4},{6,7},{7,6},{8,9},{9,8},{10,11... | collective-permute-start | bytes 442376 | tf_op jit(solution)/shard_map/ppermute | solution.py:70
  43.3 237.8 %reduce-scatter.3.cloned.1.call-start = ((), (), s32[]{:S(2)}) async-start(), calls=%async_computation.3 | async-start | bytes 10616832 | tf_op jit(solution)/shard_map/reduce_scatter | solution.py:1091
  58.4 6.8 %collective-permute-start.13 = (f32[1,1,2,4608]{3,2,1,0:T(2,128)S(1)}, f32[1,1,2,4608]{3,2,1,0:T(2,128)S(1)}, u32[]{:S(2)}, u32[]{:S(2)}) collective-permute-start(f32[1,1,2,4608]{3,2,1,0:T(2,128)S(1)} %constant_dynamic-slice_fusion.21), channel_id=1, source_target_pairs={{0,16},{2,18},{4,20},{6,22},{8,24},{10,26},{12,28},{14,30},{16,0},... | collective-permute-start | bytes 110600 | tf_op jit(solution)/shard_map/ppermute | solution.py:70
  61.9 15.8 %collective-permute-start.15 = (bf16[2,2,1,1,2,24,1536]{6,5,4,3,2,1,0:T(8,128)(2,1)S(1)}, bf16[2,2,1,1,2,24,1536]{6,5,4,3,2,1,0:T(8,128)(2,1)S(1)}, u32[]{:S(2)}, u32[]{:S(2)}) collective-permute-start(bf16[2,2,1,1,2,24,1536]{6,5,4,3,2,1,0:T(8,128)(2,1)S(1)} %pad_maximum_fusion.11), channel_id=1, source_target_pairs={{0,4},{2,6},{4,0},{6,2},{8,12},{10,14},{12,8},{14,10},{16,20},{18,... | collective-permute-start | bytes 1769480 | tf_op jit(solution)/shard_map/ppermute | solution.py:70
  62.1 15.8 %collective-permute-start.14 = (bf16[2,2,2,1,1,24,1536]{6,5,4,3,2,1,0:T(8,128)(2,1)S(1)}, bf16[2,2,2,1,1,24,1536]{6,5,4,3,2,1,0:T(8,128)(2,1)S(1)}, u32[]{:S(2)}, u32[]{:S(2)}) collective-permute-start(bf16[2,2,2,1,1,24,1536]{6,5,4,3,2,1,0:T(8,128)(2,1)S(1)} %pad_maximum_fusion.10), channel_id=1, source_target_pairs={{0,1},{1,0},{2,3},{3,2},{4,5},{5,4},{6,7},{7,6},{8,9},{9,8},{10,11... | collective-permute-start | bytes 1769480 | tf_op jit(solution)/shard_map/ppermute | solution.py:70
  62.8 30.7 %collective-permute-start.22 = (bf16[2,1,1,1,64,768]{5,4,3,2,1,0:T(8,128)(2,1)S(1)}, bf16[2,1,1,1,64,768]{5,4,3,2,1,0:T(8,128)(2,1)S(1)}, u32[]{:S(2)}, u32[]{:S(2)}) collective-permute-start(bf16[2,1,1,1,64,768]{5,4,3,2,1,0:T(8,128)(2,1)S(1)} %pad_maximum_fusion.19), channel_id=1, source_target_pairs={{0,8},{2,10},{4,12},{6,14},{8,0},{10,2},{12,4},{14,6},{16,24},{18,... | collective-permute-start | bytes 589832 | tf_op jit(solution)/shard_map/ppermute | solution.py:70
  64.4 15.7 %collective-permute-start.20 = (bf16[2,1,1,1,1,24,1536]{6,5,4,3,2,1,0:T(8,128)(2,1)S(1)}, bf16[2,1,1,1,1,24,1536]{6,5,4,3,2,1,0:T(8,128)(2,1)S(1)}, u32[]{:S(2)}, u32[]{:S(2)}) collective-permute-start(bf16[2,1,1,1,1,24,1536]{6,5,4,3,2,1,0:T(8,128)(2,1)S(1)} %pad_maximum_fusion.21), channel_id=1, source_target_pairs={{0,8},{2,10},{4,12},{6,14},{8,0},{10,2},{12,4},{14,6},{16,24},{18,... | collective-permute-start | bytes 442376 | tf_op jit(solution)/shard_map/ppermute | solution.py:70
  82.5 11.2 %collective-permute-start.21 = (bf16[2,2,1,1,1,24,1536]{6,5,4,3,2,1,0:T(8,128)(2,1)S(1)}, bf16[2,2,1,1,1,24,1536]{6,5,4,3,2,1,0:T(8,128)(2,1)S(1)}, u32[]{:S(2)}, u32[]{:S(2)}) collective-permute-start(bf16[2,2,1,1,1,24,1536]{6,5,4,3,2,1,0:T(8,128)(2,1)S(1)} %pad_maximum_fusion.17), channel_id=1, source_target_pairs={{0,4},{2,6},{4,0},{6,2},{8,12},{10,14},{12,8},{14,10},{16,20},{18,... | collective-permute-start | bytes 884744 | tf_op jit(solution)/shard_map/ppermute | solution.py:70
  93.2 20.0 %collective-permute-start.24 = (bf16[512,1536]{1,0:T(8,128)(2,1)S(1)}, bf16[512,1536]{1,0:T(8,128)(2,1)S(1)}, u32[]{:S(2)}, u32[]{:S(2)}) collective-permute-start(bf16[512,1536]{1,0:T(8,128)(2,1)S(1)} %get-tuple-element.197.refs_1_.refs_2_.refs_4_.refs_5_), channel_id=1, source_target_pairs={{0,2},{2,0},{4,6},{6,4},{8,10},{10,8},{12,14},{14,12},{16,18},{18,... | collective-permute-start | bytes 4718600 | tf_op jit(solution)/shard_map/ppermute | solution.py:70
  93.6 18.6 %collective-permute-start.23 = (bf16[2,2,1,1,64,768]{5,4,3,2,1,0:T(8,128)(2,1)S(1)}, bf16[2,2,1,1,64,768]{5,4,3,2,1,0:T(8,128)(2,1)S(1)}, u32[]{:S(2)}, u32[]{:S(2)}) collective-permute-start(bf16[2,2,1,1,64,768]{5,4,3,2,1,0:T(8,128)(2,1)S(1)} %pad_maximum_fusion.14), channel_id=1, source_target_pairs={{0,1},{1,0},{2,3},{3,2},{4,5},{5,4},{6,7},{7,6},{8,9},{9,8},{10,11... | collective-permute-start | bytes 1179656 | tf_op jit(solution)/shard_map/ppermute | solution.py:70
  113.2 21.4 %collective-permute-start.25 = (bf16[2,2,2,1,1,24,1536]{6,5,4,3,2,1,0:T(8,128)(2,1)}, bf16[2,2,2,1,1,24,1536]{6,5,4,3,2,1,0:T(8,128)(2,1)}, u32[]{:S(2)}, u32[]{:S(2)}) collective-permute-start(bf16[2,2,2,1,1,24,1536]{6,5,4,3,2,1,0:T(8,128)(2,1)} %pad_maximum_fusion.13), channel_id=1, source_target_pairs={{0,1},{1,0},{2,3},{3,2},{4,5},{5,4},{6,7},{7,6},{8,9},{9,8},{10,11... | collective-permute-start | bytes 1769480 | tf_op jit(solution)/shard_map/ppermute | solution.py:70
  115.4 20.6 %collective-permute-start.26 = (bf16[2,2,1,1,64,1536]{5,4,3,2,1,0:T(8,128)(2,1)}, bf16[2,2,1,1,64,1536]{5,4,3,2,1,0:T(8,128)(2,1)S(1)}, u32[]{:S(2)}, u32[]{:S(2)}) collective-permute-start(bf16[2,2,1,1,64,1536]{5,4,3,2,1,0:T(8,128)(2,1)} %pad_maximum_fusion.8), channel_id=1, source_target_pairs={{0,4},{2,6},{4,0},{6,2},{8,12},{10,14},{12,8},{14,10},{16,20},{18,... | collective-permute-start | bytes 2359304 | tf_op jit(solution)/shard_map/ppermute | solution.py:70
  137.4 5.5 %collective-permute-start.28 = (bf16[2,2,2,1,2,24,1536]{6,5,4,3,2,1,0:T(8,128)(2,1)S(1)}, bf16[2,2,2,1,2,24,1536]{6,5,4,3,2,1,0:T(8,128)(2,1)S(1)}, u32[]{:S(2)}, u32[]{:S(2)}) collective-permute-start(bf16[2,2,2,1,2,24,1536]{6,5,4,3,2,1,0:T(8,128)(2,1)S(1)} %pad_maximum_fusion.7), channel_id=1, source_target_pairs={{0,2},{2,0},{4,6},{6,4},{8,10},{10,8},{12,14},{14,12},{16,18},{18,... | collective-permute-start | bytes 3538952 | tf_op jit(solution)/shard_map/ppermute | solution.py:70
  142.3 17.0 %collective-permute-start.31 = (bf16[512,768]{1,0:T(8,128)(2,1)S(1)}, bf16[512,768]{1,0:T(8,128)(2,1)S(1)}, u32[]{:S(2)}, u32[]{:S(2)}) collective-permute-start(bf16[512,768]{1,0:T(8,128)(2,1)S(1)} %bitcast.96), channel_id=1, source_target_pairs={{1,2},{2,1},{5,6},{6,5},{9,10},{10,9},{13,14},{14,13},{17,18},{18,... | collective-permute-start | bytes 2359304 | tf_op jit(solution)/shard_map/ppermute | solution.py:159
  189.1 139.6 %reduce-scatter.5.cloned.1.call-start = ((), (), s32[]{:S(2)}) async-start(), calls=%async_computation.4 | async-start | bytes 1474560 | tf_op jit(solution)/shard_map/reduce_scatter | solution.py:1173
  241.9 6.2 %collective-permute-start.34 = (bf16[2,2,2,1,2,24,1536]{6,5,4,3,2,1,0:T(8,128)(2,1)}, bf16[2,2,2,1,2,24,1536]{6,5,4,3,2,1,0:T(8,128)(2,1)}, u32[]{:S(2)}, u32[]{:S(2)}) collective-permute-start(bf16[2,2,2,1,2,24,1536]{6,5,4,3,2,1,0:T(8,128)(2,1)} %constant_dynamic-slice_fusion.18), channel_id=1, source_target_pairs={{0,2},{2,0},{4,6},{6,4},{8,10},{10,8},{12,14},{14,12},{16,18},{18,... | collective-permute-start | bytes 3538952 | tf_op jit(solution)/shard_map/ppermute | solution.py:70
  243.5 7.1 %collective-permute-start.33 = (bf16[2,2,2,1,2,24,1536]{6,5,4,3,2,1,0:T(8,128)(2,1)}, bf16[2,2,2,1,2,24,1536]{6,5,4,3,2,1,0:T(8,128)(2,1)}, u32[]{:S(2)}, u32[]{:S(2)}) collective-permute-start(bf16[2,2,2,1,2,24,1536]{6,5,4,3,2,1,0:T(8,128)(2,1)} %constant_dynamic-slice_fusion.19), channel_id=1, source_target_pairs={{0,2},{2,0},{4,6},{6,4},{8,10},{10,8},{12,14},{14,12},{16,18},{18,... | collective-permute-start | bytes 3538952 | tf_op jit(solution)/shard_map/ppermute | solution.py:70
  254.0 26.7 %collective-permute-start.39 = (bf16[2,2,2,1,64,1536]{5,4,3,2,1,0:T(8,128)(2,1)}, bf16[2,2,2,1,64,1536]{5,4,3,2,1,0:T(8,128)(2,1)S(1)}, u32[]{:S(2)}, u32[]{:S(2)}) collective-permute-start(bf16[2,2,2,1,64,1536]{5,4,3,2,1,0:T(8,128)(2,1)} %constant_dynamic-slice_fusion.14), channel_id=1, source_target_pairs={{0,2},{2,0},{4,6},{6,4},{8,10},{10,8},{12,14},{14,12},{16,18},{18,... | collective-permute-start | bytes 4718600 | tf_op jit(solution)/shard_map/ppermute | solution.py:70
  255.5 23.8 %collective-permute-start.38 = (bf16[2,2,2,1,2,24,1536]{6,5,4,3,2,1,0:T(8,128)(2,1)}, bf16[2,2,2,1,2,24,1536]{6,5,4,3,2,1,0:T(8,128)(2,1)S(1)}, u32[]{:S(2)}, u32[]{:S(2)}) collective-permute-start(bf16[2,2,2,1,2,24,1536]{6,5,4,3,2,1,0:T(8,128)(2,1)} %constant_dynamic-slice_fusion.15), channel_id=1, source_target_pairs={{0,2},{2,0},{4,6},{6,4},{8,10},{10,8},{12,14},{14,12},{16,18},{18,... | collective-permute-start | bytes 3538952 | tf_op jit(solution)/shard_map/ppermute | solution.py:70
  255.7 19.8 %collective-permute-start.37 = (bf16[2,2,1,1,2,24,1536]{6,5,4,3,2,1,0:T(8,128)(2,1)S(1)}, bf16[2,2,1,1,2,24,1536]{6,5,4,3,2,1,0:T(8,128)(2,1)S(1)}, u32[]{:S(2)}, u32[]{:S(2)}) collective-permute-start(bf16[2,2,1,1,2,24,1536]{6,5,4,3,2,1,0:T(8,128)(2,1)S(1)} %constant_dynamic-slice_fusion.16), channel_id=1, source_target_pairs={{0,4},{2,6},{4,0},{6,2},{8,12},{10,14},{12,8},{14,10},{16,20},{18,... | collective-permute-start | bytes 1769480 | tf_op jit(solution)/shard_map/ppermute | solution.py:70
  262.5 15.8 %collective-permute-start.36 = (bf16[2,2,2,1,1,24,1536]{6,5,4,3,2,1,0:T(8,128)(2,1)S(1)}, bf16[2,2,2,1,1,24,1536]{6,5,4,3,2,1,0:T(8,128)(2,1)S(1)}, u32[]{:S(2)}, u32[]{:S(2)}) collective-permute-start(bf16[2,2,2,1,1,24,1536]{6,5,4,3,2,1,0:T(8,128)(2,1)S(1)} %constant_dynamic-slice_fusion.17), channel_id=1, source_target_pairs={{0,1},{1,0},{2,3},{3,2},{4,5},{5,4},{6,7},{7,6},{8,9},{9,8},{10,11... | collective-permute-start | bytes 1769480 | tf_op jit(solution)/shard_map/ppermute | solution.py:70
  282.2 28.1 %collective-permute-start.45 = (bf16[2,2,1,1,64,1536]{5,4,3,2,1,0:T(8,128)(2,1)}, bf16[2,2,1,1,64,1536]{5,4,3,2,1,0:T(8,128)(2,1)}, u32[]{:S(2)}, u32[]{:S(2)}) collective-permute-start(bf16[2,2,1,1,64,1536]{5,4,3,2,1,0:T(8,128)(2,1)} %constant_dynamic-slice_fusion.10), channel_id=1, source_target_pairs={{0,4},{2,6},{4,0},{6,2},{8,12},{10,14},{12,8},{14,10},{16,20},{18,... | collective-permute-start | bytes 2359304 | tf_op jit(solution)/shard_map/ppermute | solution.py:70
  284.1 24.9 %collective-permute-start.44 = (bf16[2,2,2,1,1,24,1536]{6,5,4,3,2,1,0:T(8,128)(2,1)}, bf16[2,2,2,1,1,24,1536]{6,5,4,3,2,1,0:T(8,128)(2,1)}, u32[]{:S(2)}, u32[]{:S(2)}) collective-permute-start(bf16[2,2,2,1,1,24,1536]{6,5,4,3,2,1,0:T(8,128)(2,1)} %constant_dynamic-slice_fusion.11), channel_id=1, source_target_pairs={{0,1},{1,0},{2,3},{3,2},{4,5},{5,4},{6,7},{7,6},{8,9},{9,8},{10,11... | collective-permute-start | bytes 1769480 | tf_op jit(solution)/shard_map/ppermute | solution.py:70
  286.3 18.9 %collective-permute-start.43 = (bf16[2,2,1,1,1,24,1536]{6,5,4,3,2,1,0:T(8,128)(2,1)}, bf16[2,2,1,1,1,24,1536]{6,5,4,3,2,1,0:T(8,128)(2,1)}, u32[]{:S(2)}, u32[]{:S(2)}) collective-permute-start(bf16[2,2,1,1,1,24,1536]{6,5,4,3,2,1,0:T(8,128)(2,1)} %constant_dynamic-slice_fusion.12), channel_id=1, source_target_pairs={{0,1},{1,0},{2,3},{3,2},{4,5},{5,4},{6,7},{7,6},{8,9},{9,8},{10,11... | collective-permute-start | bytes 884744 | tf_op jit(solution)/shard_map/ppermute | solution.py:70
  291.6 16.3 %collective-permute-start.42 = (bf16[2,2,1,1,1,24,1536]{6,5,4,3,2,1,0:T(8,128)(2,1)}, bf16[2,2,1,1,1,24,1536]{6,5,4,3,2,1,0:T(8,128)(2,1)}, u32[]{:S(2)}, u32[]{:S(2)}) collective-permute-start(bf16[2,2,1,1,1,24,1536]{6,5,4,3,2,1,0:T(8,128)(2,1)} %constant_dynamic-slice_fusion.13), channel_id=1, source_target_pairs={{0,4},{2,6},{4,0},{6,2},{8,12},{10,14},{12,8},{14,10},{16,20},{18,... | collective-permute-start | bytes 884744 | tf_op jit(solution)/shard_map/ppermute | solution.py:70
  311.7 16.9 %collective-permute-start.51 = (bf16[2,2,1,1,64,768]{5,4,3,2,1,0:T(8,128)(2,1)S(1)}, bf16[2,2,1,1,64,768]{5,4,3,2,1,0:T(8,128)(2,1)S(1)}, u32[]{:S(2)}, u32[]{:S(2)}) collective-permute-start(bf16[2,2,1,1,64,768]{5,4,3,2,1,0:T(8,128)(2,1)S(1)} %constant_dynamic-slice_fusion.6), channel_id=1, source_target_pairs={{0,1},{1,0},{2,3},{3,2},{4,5},{5,4},{6,7},{7,6},{8,9},{9,8},{10,11... | collective-permute-start | bytes 1179656 | tf_op jit(solution)/shard_map/ppermute | solution.py:70
  312.7 15.8 %collective-permute-start.50 = (bf16[2,2,1,1,1,24,1536]{6,5,4,3,2,1,0:T(8,128)(2,1)S(1)}, bf16[2,2,1,1,1,24,1536]{6,5,4,3,2,1,0:T(8,128)(2,1)S(1)}, u32[]{:S(2)}, u32[]{:S(2)}) collective-permute-start(bf16[2,2,1,1,1,24,1536]{6,5,4,3,2,1,0:T(8,128)(2,1)S(1)} %constant_dynamic-slice_fusion.7), channel_id=1, source_target_pairs={{0,4},{2,6},{4,0},{6,2},{8,12},{10,14},{12,8},{14,10},{16,20},{18,... | collective-permute-start | bytes 884744 | tf_op jit(solution)/shard_map/ppermute | solution.py:70
  314.5 8.7 %collective-permute-start.49 = (bf16[2,1,1,1,1,24,1536]{6,5,4,3,2,1,0:T(8,128)(2,1)S(1)}, bf16[2,1,1,1,1,24,1536]{6,5,4,3,2,1,0:T(8,128)(2,1)S(1)}, u32[]{:S(2)}, u32[]{:S(2)}) collective-permute-start(bf16[2,1,1,1,1,24,1536]{6,5,4,3,2,1,0:T(8,128)(2,1)S(1)} %constant_dynamic-slice_fusion.8), channel_id=1, source_target_pairs={{0,8},{2,10},{4,12},{6,14},{8,0},{10,2},{12,4},{14,6},{16,24},{18,... | collective-permute-start | bytes 442376 | tf_op jit(solution)/shard_map/ppermute | solution.py:70
  315.0 6.8 %collective-permute-start.46 = (f32[2,2,1,1,4608]{4,3,2,1,0:T(1,128)S(1)}, f32[2,2,1,1,4608]{4,3,2,1,0:T(1,128)S(1)}, u32[]{:S(2)}, u32[]{:S(2)}) collective-permute-start(f32[2,2,1,1,4608]{4,3,2,1,0:T(1,128)S(1)} %pad_maximum_fusion.24), channel_id=1, source_target_pairs={{0,4},{2,6},{4,0},{6,2},{8,12},{10,14},{12,8},{14,10},{16,20},{18,... | collective-permute-start | bytes 221192 | tf_op jit(solution)/shard_map/ppermute | solution.py:70
  315.4 8.5 %collective-permute-start.48 = (bf16[2,1,1,1,1,24,1536]{6,5,4,3,2,1,0:T(8,128)(2,1)S(1)}, bf16[2,1,1,1,1,24,1536]{6,5,4,3,2,1,0:T(8,128)(2,1)S(1)}, u32[]{:S(2)}, u32[]{:S(2)}) collective-permute-start(bf16[2,1,1,1,1,24,1536]{6,5,4,3,2,1,0:T(8,128)(2,1)S(1)} %constant_dynamic-slice_fusion.9), channel_id=1, source_target_pairs={{0,8},{2,10},{4,12},{6,14},{8,0},{10,2},{12,4},{14,6},{16,24},{18,... | collective-permute-start | bytes 442376 | tf_op jit(solution)/shard_map/ppermute | solution.py:70
  330.4 11.8 %collective-permute-start.55 = (bf16[2,1,1,1,64,768]{5,4,3,2,1,0:T(8,128)(2,1)}, bf16[2,1,1,1,64,768]{5,4,3,2,1,0:T(8,128)(2,1)}, u32[]{:S(2)}, u32[]{:S(2)}) collective-permute-start(bf16[2,1,1,1,64,768]{5,4,3,2,1,0:T(8,128)(2,1)} %constant_dynamic-slice_fusion.2), channel_id=1, source_target_pairs={{0,8},{2,10},{4,12},{6,14},{8,0},{10,2},{12,4},{14,6},{16,24},{18,... | collective-permute-start | bytes 589832 | tf_op jit(solution)/shard_map/ppermute | solution.py:70
  331.6 9.6 %collective-permute-start.54 = (bf16[2,1,1,1,1,24,1536]{6,5,4,3,2,1,0:T(8,128)(2,1)}, bf16[2,1,1,1,1,24,1536]{6,5,4,3,2,1,0:T(8,128)(2,1)}, u32[]{:S(2)}, u32[]{:S(2)}) collective-permute-start(bf16[2,1,1,1,1,24,1536]{6,5,4,3,2,1,0:T(8,128)(2,1)} %constant_dynamic-slice_fusion.3), channel_id=1, source_target_pairs={{0,8},{2,10},{4,12},{6,14},{8,0},{10,2},{12,4},{14,6},{16,24},{18,... | collective-permute-start | bytes 442376 | tf_op jit(solution)/shard_map/ppermute | solution.py:70
  333.1 6.2 %collective-permute-start.53 = (bf16[1,1,1,1,1,24,1536]{6,5,4,3,2,1,0:T(8,128)(2,1)S(1)}, bf16[1,1,1,1,1,24,1536]{6,5,4,3,2,1,0:T(8,128)(2,1)}, u32[]{:S(2)}, u32[]{:S(2)}) collective-permute-start(bf16[1,1,1,1,1,24,1536]{6,5,4,3,2,1,0:T(8,128)(2,1)S(1)} %constant_dynamic-slice_fusion.4), channel_id=1, source_target_pairs={{0,16},{2,18},{4,20},{6,22},{8,24},{10,26},{12,28},{14,30},{16,0},... | collective-permute-start | bytes 221192 | tf_op jit(solution)/shard_map/ppermute | solution.py:70
  333.8 6.5 %collective-permute-start.52 = (bf16[1,1,1,1,1,24,1536]{6,5,4,3,2,1,0:T(8,128)(2,1)S(1)}, bf16[1,1,1,1,1,24,1536]{6,5,4,3,2,1,0:T(8,128)(2,1)}, u32[]{:S(2)}, u32[]{:S(2)}) collective-permute-start(bf16[1,1,1,1,1,24,1536]{6,5,4,3,2,1,0:T(8,128)(2,1)S(1)} %constant_dynamic-slice_fusion.5), channel_id=1, source_target_pairs={{0,16},{2,18},{4,20},{6,22},{8,24},{10,26},{12,28},{14,30},{16,0},... | collective-permute-start | bytes 221192 | tf_op jit(solution)/shard_map/ppermute | solution.py:70
  343.2 6.1 %collective-permute-start.56 = (bf16[1,1,1,1,1,24,1536]{6,5,4,3,2,1,0:T(8,128)(2,1)S(1)}, bf16[1,1,1,1,1,24,1536]{6,5,4,3,2,1,0:T(8,128)(2,1)S(1)}, u32[]{:S(2)}, u32[]{:S(2)}) collective-permute-start(bf16[1,1,1,1,1,24,1536]{6,5,4,3,2,1,0:T(8,128)(2,1)S(1)} %constant_dynamic-slice_fusion.1), channel_id=1, source_target_pairs={{0,16},{2,18},{4,20},{6,22},{8,24},{10,26},{12,28},{14,30},{16,0},... | collective-permute-start | bytes 221192 | tf_op jit(solution)/shard_map/ppermute | solution.py:70
  345.1 7.1 %collective-permute-start.57 = (bf16[1,1,1,1,64,768]{5,4,3,2,1,0:T(8,128)(2,1)S(1)}, bf16[1,1,1,1,64,768]{5,4,3,2,1,0:T(8,128)(2,1)S(1)}, u32[]{:S(2)}, u32[]{:S(2)}) collective-permute-start(bf16[1,1,1,1,64,768]{5,4,3,2,1,0:T(8,128)(2,1)S(1)} %constant_dynamic-slice_fusion), channel_id=1, source_target_pairs={{0,16},{2,18},{4,20},{6,22},{8,24},{10,26},{12,28},{14,30},{16,0},... | collective-permute-start | bytes 294920 | tf_op jit(solution)/shard_map/ppermute | solution.py:70
  346.3 48.5 %collective-permute-start.69 = (bf16[512,768]{1,0:T(8,128)(2,1)}, bf16[512,768]{1,0:T(8,128)(2,1)}, u32[]{:S(2)}, u32[]{:S(2)}) collective-permute-start(bf16[512,768]{1,0:T(8,128)(2,1)} %get-tuple-element.281), channel_id=1, source_target_pairs={{1,2},{2,1},{5,6},{6,5},{9,10},{10,9},{13,14},{14,13},{17,18},{18,... | collective-permute-start | bytes 2359304 | tf_op jit(solution)/shard_map/ppermute | solution.py:159
  347.8 49.1 %collective-permute-start.68 = (bf16[512,768]{1,0:T(8,128)(2,1)S(1)}, bf16[512,768]{1,0:T(8,128)(2,1)}, u32[]{:S(2)}, u32[]{:S(2)}) collective-permute-start(bf16[512,768]{1,0:T(8,128)(2,1)S(1)} %copy-done.33), channel_id=1, source_target_pairs={{1,2},{2,1},{5,6},{6,5},{9,10},{10,9},{13,14},{14,13},{17,18},{18,... | collective-permute-start | bytes 2359304 | tf_op jit(solution)/shard_map/ppermute | solution.py:159
  364.1 5.5 %collective-permute-start.61 = (f32[184,128]{1,0:T(8,128)S(1)}, f32[184,128]{1,0:T(8,128)S(1)}, u32[]{:S(2)}, u32[]{:S(2)}) collective-permute-start(f32[184,128]{1,0:T(8,128)S(1)} %add.462), channel_id=1, source_target_pairs={{0,16},{2,18},{4,20},{6,22},{8,24},{10,26},{12,28},{14,30},{16,0},... | collective-permute-start | bytes 282632 | tf_op jit(solution)/shard_map/ppermute | solution.py:70
  (101 other events, 561.0 us)
Sparse Core Ops, SparseCore 0:
  43.5 100.1 all-gather.1
  189.2 79.2 reduce-scatter.2
  292.3 30.8 reduce-scatter.4
